TPU v7x, 512 devices: a whole 4x4x16 slice. The times are simulated.
512 devices in a mesh: box: 64 (over y, z_lo, core), ang: 8 (over z_hi, x).
Axes of the slice: x: 4, y: 4, z: 16 (z_hi: 2, z_lo: 8; z = z_hi * 8 + z_lo), core: 2. Of those that a mesh axis runs over, the one named last changes fastest.
Arguments:
- coeffs: bfloat16 [8, 576, 2, 8192], P('ang', None, None, 'box'), may hold values from -6 to 6
- freqs: bfloat16 [8, 5, 2, 8192], P('ang', None, None, 'box'), may hold values from -6 to 6
- nodes: float32 [4, 3, 2, 576], replicated, may hold values from -0.5 to 0.5
- centres: float32 [4, 3, 2, 64], replicated, may hold values from -2 to 2
- interp: bfloat16 [2, 576, 576], replicated, may hold values from -0.1875 to 0.1875
- evaluate: bfloat16 [1024, 576], replicated, may hold values from -0.09375 to 0.09375
Outputs:
- image_slice: float32 [1024, 8192], P('ang', 'box')
All inputs are finite; a program needn't handle non-finite values.
Results may differ from a plain program's by a relative error of at most 0.015.
Values may be sent and summed in bfloat16 or wider, within the bound.
No kernel may reach another device: no remote copies, remote signals or barrier semaphores. Data moves between devices by JAX's collectives and lax.ppermute only.
A program may use at most 192 MiB of HBM per device.

v0:
```python
import jax
import jax.numpy as jnp
from jax import lax
from jax.sharding import PartitionSpec as P


def from_partner(block, axis, bit):
    count = lax.axis_size(axis)
    route = []
    for low in range(count):
        high = low | 1 << bit
        if high != low and high < count:
            route += [(low, high), (high, low)]
    return lax.ppermute(block, axis, route)


def angle(rel_two, cen_two, freq_two):
    first = (rel_two[0][:, None] + cen_two[0][None, :]) * freq_two[0][None, :]
    second = (rel_two[1][:, None] + cen_two[1][None, :]) * freq_two[1][None, :]
    return first + second


def rotate(values, phase):
    real_part = values[:, 0].astype(jnp.float32)
    imag_part = values[:, 1].astype(jnp.float32)
    cosine = jnp.cos(phase)
    sine = jnp.sin(phase)
    return jnp.stack(
        [cosine * real_part - sine * imag_part, sine * real_part + cosine * imag_part], axis=1
    )


def section_core(own, other, bits, rel_s, cen_s, freq_s, interp):
    coeff_count = own.shape[0]
    width = own.shape[2]
    lower_self = (bits == 0)[None, None, :]
    lower = jnp.where(lower_self, own, other)
    upper = jnp.where(lower_self, other, own)
    w_low = rotate(lower, -angle(rel_s[0], cen_s[0], freq_s)).astype(jnp.bfloat16)
    w_high = rotate(upper, -angle(rel_s[1], cen_s[1], freq_s)).astype(jnp.bfloat16)
    total = jnp.dot(
        interp[0], w_low.reshape(coeff_count, 2 * width), preferred_element_type=jnp.float32
    )
    total = total + jnp.dot(
        interp[1], w_high.reshape(coeff_count, 2 * width), preferred_element_type=jnp.float32
    )
    return rotate(total.reshape(coeff_count, 2, width), angle(rel_s[2], cen_s[2], freq_s)).astype(
        jnp.bfloat16
    )


def body(coeffs, freqs, nodes, centres, interp, evaluate):
    field = coeffs[0]
    freq = freqs[0]
    levels = nodes.shape[0]
    width = field.shape[2]
    mine = lax.axis_index("box")
    own_cen = lax.dynamic_slice_in_dim(centres, mine, 1, 3)
    own_cen = jnp.broadcast_to(own_cen, centres.shape[:3] + (width,))
    own_box = jnp.full((width,), mine, jnp.int32)
    for level in range(levels):
        other = from_partner(field, "box", level)
        field = section_core(
            field,
            other,
            own_box >> level & 1,
            nodes[level],
            own_cen[level],
            freq[level].astype(jnp.float32),
            interp,
        )
    phase = angle(nodes[levels - 1, 2], own_cen[levels - 1, 2], freq[levels].astype(jnp.float32))
    values = (
        jnp.cos(phase) * field[:, 0].astype(jnp.float32)
        - jnp.sin(phase) * field[:, 1].astype(jnp.float32)
    ).astype(jnp.bfloat16)
    return lax.psum_scatter(
        jnp.dot(evaluate, values, preferred_element_type=jnp.float32),
        "ang",
        scatter_dimension=0,
        tiled=True,
    )


def solution(mesh):
    return jax.shard_map(
        body,
        mesh=mesh,
        in_specs=(P("ang", None, None, "box"), P("ang", None, None, "box"), P(), P(), P(), P()),
        out_specs=P("ang", "box"),
        check_vma=False,
    )
```

profile of v0, /device:TPU:1, one launch (start us, length us, event | category | flops | bytes accessed | tf_op | source)
XLA Modules:
  0.0 248.4 jit_solution(11731679123485992226)
XLA Ops:
  6.5 0.0 copy-start
  6.5 0.0 reduce-scatter.2.cloned.1.call-start
  6.5 1.1 copy.90
  7.6 8.8 %collective-permute-start = (bf16[576,2,128]{2,0,1:T(8,128)(2,1)S(1)}, bf16[576,2,128]{2,0,1:T(8,128)(2,1)S(1)}, u32[]{:S(2)}, u32[]{:S(2)}) collective-permute-start(bf16[576,2,128]{2,0,1:T(8,128)(2,1)S(1)} %bitcast.163), channel_id=1, source_target_pairs={{0,8},{8,0},{16,24},{24,16},{32,40},{40,32},{48,56},{56,48},{64,72... | collective-permute-start | bytes 884744 | tf_op jit(solution)/shard_map/ppermute | solution.py:14
  16.4 0.8 constant_dynamic-slice_fusion.18
  17.2 0.1 copy.18
  17.4 0.7 fusion.112
  18.0 1.3 slice_convert_fusion.4
  19.3 1.6 constant_dynamic-slice_fusion.14
  21.0 7.2 %add_reduce_fusion.24 = (f32[576]{0:T(1024)}, f32[576]{0:T(1024)S(1)}, f32[576]{0:T(1024)S(1)}, f32[576]{0:T(1024)S(1)}, f32[576]{0:T(1024)S(1)}, /*index=5*/f32...) fusion(f32[4,3,2,576]{3,2,1,0:T(2,128)} %param.8, f32[]{:T(128)} %bitcast.3, f32[]{:T(128)} %bitcast.28, ...), kind=kLoop, calls=%fused_computation.229 | loop fusion | flops 5184 | bytes 41508 | tf_op jit(solution)/shard_map/add | solution.py:19
  28.2 7.0 %add_reduce_fusion.25 = (f32[576]{0:T(1024)}, f32[576]{0:T(1024)}, f32[576]{0:T(1024)}, f32[576]{0:T(1024)}, f32[576]{0:T(1024)}, /*index=5*/f32[576]{0:T(1024)}, f32[576]{0:T(1024)}, f32[576]{0:T(1024)S(1)}, f32[576]{0:T(1024)S(1)}) fusion(f32[4,3,2,576]{3,2,1,0:T(2,128)} %param.8, f32[]{:T(128)} %bitcast.1, f32[]{:T(128)} %bitcast.5, f32[]{:T(128)} %bitcast.7, ...), kind=kLoop, calls=%fused_computation.230 | loop fusion | flops 5184 | bytes 39204 | tf_op jit(solution)/shard_map/add | solution.py:18
  35.2 0.0 collective-permute-done
  35.2 1.0 broadcast_select_fusion
  36.2 0.0 copy-start.1
  36.2 3.0 %fusion.29 = (bf16[576,1,128]{2,0,1:T(8,128)(2,1)S(1)}, bf16[576,1,128]{2,0,1:T(8,128)(2,1)S(1)}, bf16[576,1,128]{2,0,1:T(8,128)(2,1)S(1)}, bf16[576,1,128]{2,0,1:T(8,128)(2,1)S(1)}) fusion(f32[576]{0:T(1024)S(1)} %get-tuple-element.12, f32[576]{0:T(1024)S(1)} %get-tuple-element.13, f32[128]{0:T(128)S(1)} %get-tuple-element.111, ...), kind=kLoop, calls=%fused_computation.66 | loop fusion | flops 2064384 | bytes 1189888 | tf_op jit(solution)/shard_map/convert.22
  39.3 0.1 maximum_bitcast_fusion
  39.4 0.0 copy-done.1
  39.4 0.4 fusion.8
  39.8 1.2 fusion
  41.0 1.4 reshape.2964
  42.3 0.5 fusion.111
  42.8 1.5 subtract_convert_fusion.3
  44.3 1.9 collective-permute-start.1
  46.3 0.7 slice_bitcast_fusion.3
  47.0 7.8 %collective-permute-done.1 = bf16[576,2,128]{2,0,1:T(8,128)(2,1)S(1)} collective-permute-done((bf16[576,2,128]{2,0,1:T(8,128)(2,1)S(1)}, bf16[576,2,128]{2,0,1:T(8,128)(2,1)S(1)}, u32[]{:S(2)}, u32[]{:S(2)}) %collective-permute-start.1) | collective-permute-done | bytes 294944 | tf_op jit(solution)/shard_map/ppermute | solution.py:14
  54.9 3.6 %fusion.37 = (bf16[576,1,128]{2,0,1:T(8,128)(2,1)S(1)}, bf16[576,1,128]{2,0,1:T(8,128)(2,1)S(1)}, bf16[576,1,128]{2,0,1:T(8,128)(2,1)S(1)}, bf16[576,1,128]{2,0,1:T(8,128)(2,1)S(1)}) fusion(f32[576]{0:T(1024)} %get-tuple-element.10, f32[576]{0:T(1024)} %get-tuple-element.11, f32[128]{0:T(128)S(1)} %get-tuple-element.113, f32[128]{0:T(128)S(1)} %get-tuple-element.112, ...), kind=kLoop, calls=%fused_computation.74 | loop fusion | flops 2064384 | bytes 1189888 | tf_op jit(solution)/shard_map/convert.16
  58.5 0.4 fusion.10
  58.9 0.0 copy-done.8
  58.9 0.0 copy-done.10
  58.9 1.2 fusion.1
  60.2 1.4 reshape.2965
  61.5 0.0 copy-start.15
  61.5 0.5 fusion.110
  62.0 0.0 copy-start.6
  62.0 1.5 subtract_convert_fusion.2
  63.5 1.9 collective-permute-start.2
  65.5 5.7 %add_reduce_fusion.1 = (f32[576]{0:T(1024)S(1)}, f32[576]{0:T(1024)S(1)}, f32[576]{0:T(1024)S(1)}, f32[576]{0:T(1024)S(1)}, f32[576]{0:T(1024)S(1)}, /*index=5*/...) fusion(f32[4,3,2,576]{3,2,1,0:T(2,128)} %param.8, f32[]{:T(128)} %bitcast.41, f32[]{:T(128)} %bitcast.16, f32[]{:T(128)} %bitcast.15, ...), kind=kLoop, calls=%fused_computation.206 | loop fusion | flops 4608 | bytes 36896 | tf_op jit(solution)/shard_map/add | solution.py:18
  71.2 10.4 %collective-permute-done.2 = bf16[576,2,128]{2,0,1:T(8,128)(2,1)S(1)} collective-permute-done((bf16[576,2,128]{2,0,1:T(8,128)(2,1)S(1)}, bf16[576,2,128]{2,0,1:T(8,128)(2,1)S(1)}, u32[]{:S(2)}, u32[]{:S(2)}) %collective-permute-start.2) | collective-permute-done | bytes 294944 | tf_op jit(solution)/shard_map/ppermute | solution.py:14
  81.6 3.0 %fusion.45 = (bf16[576,1,128]{2,0,1:T(8,128)(2,1)S(1)}, bf16[576,1,128]{2,0,1:T(8,128)(2,1)S(1)}, bf16[576,1,128]{2,0,1:T(8,128)(2,1)S(1)}, bf16[576,1,128]{2,0,1:T(8,128)(2,1)S(1)}) fusion(f32[576]{0:T(1024)S(1)} %copy-done.6, f32[576]{0:T(1024)S(1)} %copy-done.7, f32[128]{0:T(128)S(1)} %get-tuple-element.115, f32[128]{0:T(128)S(1)} %get-tuple-element.114, ...), kind=kLoop, calls=%fused_computation.82 | loop fusion | flops 2064384 | bytes 1189888 | tf_op jit(solution)/shard_map/convert.10
  84.6 0.4 fusion.12
  85.0 1.2 fusion.2
  86.3 1.4 reshape.2966
  87.6 0.5 fusion.109
  88.1 1.5 subtract_convert_fusion.1
  89.6 3.9 %collective-permute-start.3 = (bf16[576,2,128]{2,0,1:T(8,128)(2,1)S(1)}, bf16[576,2,128]{2,0,1:T(8,128)(2,1)S(1)}, u32[]{:S(2)}, u32[]{:S(2)}) collective-permute-start(bf16[576,2,128]{2,0,1:T(8,128)(2,1)S(1)} %pad_maximum_fusion.2), channel_id=1, source_target_pairs={{0,64},{64,0},{8,72},{72,8},{16,80},{80,16},{24,88},{88,24},{32,96... | collective-permute-start | bytes 884744 | tf_op jit(solution)/shard_map/ppermute | solution.py:14
  93.5 0.5 slice_bitcast_fusion.7
  94.0 1.3 slice_bitcast_fusion.9
  95.3 25.3 %collective-permute-done.3 = bf16[576,2,128]{2,0,1:T(8,128)(2,1)S(1)} collective-permute-done((bf16[576,2,128]{2,0,1:T(8,128)(2,1)S(1)}, bf16[576,2,128]{2,0,1:T(8,128)(2,1)S(1)}, u32[]{:S(2)}, u32[]{:S(2)}) %collective-permute-start.3) | collective-permute-done | bytes 294944 | tf_op jit(solution)/shard_map/ppermute | solution.py:14
  120.7 3.5 %fusion.53 = (bf16[576,1,128]{2,0,1:T(8,128)(2,1)S(1)}, bf16[576,1,128]{2,0,1:T(8,128)(2,1)S(1)}, bf16[576,1,128]{2,0,1:T(8,128)(2,1)S(1)}, bf16[576,1,128]{2,0,1:T(8,128)(2,1)S(1)}) fusion(f32[576]{0:T(1024)S(1)} %get-tuple-element.30, f32[576]{0:T(1024)S(1)} %get-tuple-element.23, f32[128]{0:T(128)} %get-tuple-element.117, f32[128]{0:T(128)} %get-tuple-element.116, ...), kind=kLoop, calls=%fused_computation.90 | loop fusion | flops 2064384 | bytes 1189888 | tf_op jit(solution)/shard_map/convert.4
  124.2 0.4 fusion.14
  124.6 0.4 fusion.3
  125.0 0.0 copy-start.3
  125.0 0.0 copy-start.4
  125.0 0.0 copy-start.5
  125.0 0.0 copy-start.12
  125.0 0.0 copy-start.13
  125.0 0.0 copy-start.16
  125.0 0.0 copy-start.17
  125.1 0.3 reshape.2967
  125.4 0.5 fusion.108
  125.9 3.4 %convolution_bitcast_fusion = f32[1024,128]{0,1:T(8,128)} fusion(bf16[1024,576]{0,1:T(8,128)(2,1)S(1)} %copy-done, f32[576,1,128]{2,0,1:T(8,128)S(1)} %bitcast.156, f32[576,1,128]{2,0,1:T(8,128)S(1)} %bitcast.155, f32[128]{0:T(128)S(1)} %copy-done.13, f32[576]{0:T(1024)S(1)} %copy-done.5, f32[128]{0:T(128)S(1)} %copy-done.12, f32[576]{0:T(1024)S(1)} %copy-done.4, ...), kind=kOutput, calls=%fused_computation.8 | convolution fusion | flops 152469504 | bytes 2305024 | tf_op jit(solution)/shard_map/dot_general | solution.py:78
  129.3 0.0 reduce-scatter.2.cloned.1.call-update
  129.4 110.6 %reduce-scatter.2.cloned.1.call-done = f32[128,128]{0,1:T(8,128)} async-done(((f32[1024,128]{0,1:T(8,128)}), f32[128,128]{0,1:T(8,128)}) %reduce-scatter.2.cloned.1.call-update) | async-done | bytes 65552 | tf_op jit(solution)/shard_map/reduce_scatter | solution.py:77
  240.0 1.6 copy.36
  (30 shorter events, 0.3 us)
Async XLA Ops:
  6.5 119.3 %copy-start = (bf16[1024,576]{0,1:T(8,128)(2,1)S(1)}, bf16[1024,576]{0,1:T(8,128)(2,1)}, u32[]{:S(2)}) copy-start(bf16[1024,576]{0,1:T(8,128)(2,1)} %param.11) | copy-start | bytes 3538948
  6.5 233.4 %reduce-scatter.2.cloned.1.call-start = ((), (), s32[]{:S(2)}) async-start(), calls=%async_computation.1 | async-start | bytes 589824 | tf_op jit(solution)/shard_map/reduce_scatter | solution.py:77
  7.6 27.6 %collective-permute-start = (bf16[576,2,128]{2,0,1:T(8,128)(2,1)S(1)}, bf16[576,2,128]{2,0,1:T(8,128)(2,1)S(1)}, u32[]{:S(2)}, u32[]{:S(2)}) collective-permute-start(bf16[576,2,128]{2,0,1:T(8,128)(2,1)S(1)} %bitcast.163), channel_id=1, source_target_pairs={{0,8},{8,0},{16,24},{24,16},{32,40},{40,32},{48,56},{56,48},{64,72... | collective-permute-start | bytes 884744 | tf_op jit(solution)/shard_map/ppermute | solution.py:14
  36.2 3.1 %copy-start.1 = (bf16[2,576,576]{2,1,0:T(8,128)(2,1)S(1)}, bf16[2,576,576]{2,1,0:T(8,128)(2,1)}, u32[]{:S(2)}) copy-start(bf16[2,576,576]{2,1,0:T(8,128)(2,1)} %param.10) | copy-start | bytes 3981316
  44.3 10.5 %collective-permute-start.1 = (bf16[576,2,128]{2,0,1:T(8,128)(2,1)S(1)}, bf16[576,2,128]{2,0,1:T(8,128)(2,1)S(1)}, u32[]{:S(2)}, u32[]{:S(2)}) collective-permute-start(bf16[576,2,128]{2,0,1:T(8,128)(2,1)S(1)} %pad_maximum_fusion), channel_id=1, source_target_pairs={{0,16},{16,0},{8,24},{24,8},{32,48},{48,32},{40,56},{56,40},{64,80... | collective-permute-start | bytes 884744 | tf_op jit(solution)/shard_map/ppermute | solution.py:14
  47.0 11.9 %copy-start.8 = (f32[128]{0:T(128)}, f32[128]{0:T(128)S(1)}, u32[]{:S(2)}) copy-start(f32[128]{0:T(128)S(1)} %get-tuple-element.112) | copy-start | bytes 1540
  47.0 11.9 %copy-start.10 = (f32[128]{0:T(128)}, f32[128]{0:T(128)S(1)}, u32[]{:S(2)}) copy-start(f32[128]{0:T(128)S(1)} %get-tuple-element.113) | copy-start | bytes 1540
  60.2 1.9 copy-start.9
  60.2 1.9 copy-start.11
  61.5 9.6 %copy-start.15 = (f32[1,1,2,128]{3,2,1,0:T(2,128)S(1)}, f32[1,1,2,128]{3,2,1,0:T(2,128)}, u32[]{:S(2)}) copy-start(f32[1,1,2,128]{3,2,1,0:T(2,128)} %get-tuple-element.96) | copy-start | bytes 3076
  62.0 19.6 %copy-start.6 = (f32[576]{0:T(1024)S(1)}, f32[576]{0:T(1024)}, u32[]{:S(2)}) copy-start(f32[576]{0:T(1024)} %get-tuple-element.8) | copy-start | bytes 6916
  62.0 19.6 %copy-start.7 = (f32[576]{0:T(1024)S(1)}, f32[576]{0:T(1024)}, u32[]{:S(2)}) copy-start(f32[576]{0:T(1024)} %get-tuple-element.9) | copy-start | bytes 6916
  63.5 18.0 %collective-permute-start.2 = (bf16[576,2,128]{2,0,1:T(8,128)(2,1)S(1)}, bf16[576,2,128]{2,0,1:T(8,128)(2,1)S(1)}, u32[]{:S(2)}, u32[]{:S(2)}) collective-permute-start(bf16[576,2,128]{2,0,1:T(8,128)(2,1)S(1)} %pad_maximum_fusion.1), channel_id=1, source_target_pairs={{0,32},{32,0},{8,40},{40,8},{16,48},{48,16},{24,56},{56,24},{64,96... | collective-permute-start | bytes 884744 | tf_op jit(solution)/shard_map/ppermute | solution.py:14
  87.6 5.9 %copy-start.14 = (f32[1,1,2,128]{3,2,1,0:T(2,128)S(1)}, f32[1,1,2,128]{3,2,1,0:T(2,128)}, u32[]{:S(2)}) copy-start(f32[1,1,2,128]{3,2,1,0:T(2,128)} %get-tuple-element.97) | copy-start | bytes 3076
  89.6 31.0 %collective-permute-start.3 = (bf16[576,2,128]{2,0,1:T(8,128)(2,1)S(1)}, bf16[576,2,128]{2,0,1:T(8,128)(2,1)S(1)}, u32[]{:S(2)}, u32[]{:S(2)}) collective-permute-start(bf16[576,2,128]{2,0,1:T(8,128)(2,1)S(1)} %pad_maximum_fusion.2), channel_id=1, source_target_pairs={{0,64},{64,0},{8,72},{72,8},{16,80},{80,16},{24,88},{88,24},{32,96... | collective-permute-start | bytes 884744 | tf_op jit(solution)/shard_map/ppermute | solution.py:14
  125.0 0.9 copy-start.2
  125.0 0.9 copy-start.3
  125.0 0.9 copy-start.4
  125.0 0.9 copy-start.5
  125.0 0.9 copy-start.12
  125.0 0.9 copy-start.13
  125.0 0.9 copy-start.16
  125.0 0.9 copy-start.17
Sparse Core Ops, SparseCore 0:
  129.5 110.4 reduce-scatter.1
where the time goes:
time: 250 us; the launch traced here: 248 us
  waiting for transfers between devices  154 us (62%)
  other arithmetic  40.1 us (16%)
  starting transfers between devices  16.5 us (7%)
  local copies, waits for them, and re-layouts  14.7 us (6%)
  between operations  13.9 us (6%)
  matrix products  9.03 us (4%)
    reduce_scatter x1, waiting for transfers between devices, body(): lax.psum_scatter(jnp.dot(evaluate, values, preferred_element_type=jnp.flo...  111 us
    ppermute x4, waiting for transfers between devices, from_partner(): return lax.ppermute(block, axis, route)  43.5 us
    another operation x7, other arithmetic  17.6 us
    ppermute x4, starting transfers between devices, from_partner(): return lax.ppermute(block, axis, route)  16.5 us
    add x2, other arithmetic, angle(): first = (rel_two[0][:, None] + cen_two[0][None, :]) * freq_two[0][None, :]  12.7 us
    add x1, other arithmetic, angle(): second = (rel_two[1][:, None] + cen_two[1][None, :]) * freq_two[1][None, :]  7.22 us
  transfers between devices with their start and end apart: 5, of which 4 were waited for; matrix products, arithmetic and copies ran while one was open for 11% of the time, Pallas kernels for 0%

commit v1 on v0

v1 whole, which is shorter than its diff:
```python
import jax
import jax.numpy as jnp
import numpy as np
from jax import lax
from jax.experimental import pallas as pl
from jax.experimental.pallas import tpu as pltpu
from jax.sharding import Mesh, PartitionSpec as P

AXES = ("y", "z4", "z2", "z1", "c", "zh", "x")
SIZES = (4, 2, 2, 2, 2, 2, 4)
NEAR = ("z2", "z1", "c", "x")
FAR = ("z4",) + NEAR
ALL = ("z4", "z2", "z1", "c", "zh", "x")
K = 576
COLS = 128
PIX = 1024
F32 = jnp.float32
BF16 = jnp.bfloat16

COS = (
    0.999999989059023,
    -19.739204499453944,
    64.9391174598965,
    -85.45013953089278,
    60.16763095097771,
    -25.96759924841038,
    6.5286581610231424,
)
SIN = (
    6.283184916495431,
    -41.34158923268858,
    81.59994332978287,
    -76.61447253124996,
    41.34288235456833,
    -12.471243535026977,
)


def horner(coefficients, u):
    total = u * coefficients[-1] + coefficients[-2]
    for value in coefficients[-3::-1]:
        total = total * u + value
    return total


def cos_sin(turns):
    r = turns - jnp.floor(turns + 0.5)
    u = r * r
    return horner(COS, u), r * horner(SIN, u)


def trig_kernel(where_ref, freq_ref, nodes_ref, cen_ref, cos_ref, sin_ref, g_ref, c_ref):
    base = where_ref[0] * 16
    half = where_ref[1]
    row = lax.broadcasted_iota(jnp.int32, (COLS, 64), 0) // 16
    lane = lax.broadcasted_iota(jnp.int32, (COLS, 64), 1)
    for t in range(2):
        hot = jnp.where(lane == row + (base + t * 8), 1.0, 0.0).astype(F32)
        c_ref[t] = lax.dot_general(
            hot,
            cen_ref[...],
            (((1,), (1,)), ((), ())),
            precision=lax.Precision.HIGHEST,
            preferred_element_type=F32,
        )
        g_ref[t] = freq_ref[t].astype(F32) * (0.5 / np.pi)

    def node(level, kind, d):
        i = (level * 3 + kind) * 2 + d
        return nodes_ref[i : i + 1, :]

    def cen(block, level, kind, d):
        i = (level * 3 + kind) * 2 + d
        return block[:, i : i + 1]

    def fr(block, level, d):
        i = level * 2 + d
        return block[:, i : i + 1]

    low_side = half == 0

    @pl.loop(0, 16)
    def _(i):
        here = pl.ds(pl.multiple_of(i * 8, 8), 8)

        def store(index, turns):
            c, s = cos_sin(turns)
            cos_ref[index, here, :] = c
            sin_ref[index, here, :] = s

        def phase(level, kind, g, cc):
            fx, fy = fr(g, level, 0), fr(g, level, 1)
            const = cen(cc, level, kind, 0) * fx + cen(cc, level, kind, 1) * fy
            return node(level, kind, 0) * fx + node(level, kind, 1) * fy + const

        g_own, c_own = g_ref[half, here, :], c_ref[half, here, :]
        for kind in range(2):
            store(kind, -phase(0, kind, g_own, c_own))
        for level in range(1, 3):
            bit = 2 << level
            for kind in range(2):
                src = (i & ~bit) | (bit * kind)
                there = pl.ds(pl.multiple_of(src * 8, 8), 8)
                up = phase(level - 1, 2, g_ref[half, there, :], c_ref[half, there, :])
                store(2 * level + kind, up - phase(level, kind, g_own, c_own))
        up = phase(2, 2, g_own, c_own)
        for t in range(2):
            g, cc = g_ref[t, here, :], c_ref[t, here, :]
            down = jnp.where(low_side, phase(3, 0, g, cc), phase(3, 1, g, cc))
            store(6 + t, up - down)
            fx = fr(g, 3, 0) + fr(g, 4, 0)
            fy = fr(g, 3, 1) + fr(g, 4, 1)
            const = cen(cc, 3, 2, 0) * fx + cen(cc, 3, 2, 1) * fy
            store(8 + t, node(3, 2, 0) * fx + node(3, 2, 1) * fy + const)


def trig(where, freq, nodes, cen):
    n = 10 * COLS * K
    return pl.pallas_call(
        trig_kernel,
        out_shape=[jax.ShapeDtypeStruct((10, COLS, K), F32)] * 2,
        in_specs=[pl.BlockSpec(memory_space=pltpu.SMEM)]
        + [pl.BlockSpec(memory_space=pltpu.VMEM)] * 3,
        out_specs=[pl.BlockSpec(memory_space=pltpu.VMEM)] * 2,
        scratch_shapes=[pltpu.VMEM((2, COLS, 10), F32), pltpu.VMEM((2, COLS, 24), F32)],
        compiler_params=pltpu.CompilerParams(vmem_limit_bytes=24 * 2**20),
        cost_estimate=pl.CostEstimate(flops=n * 40, bytes_accessed=n * 8, transcendentals=0),
        name="trig",
    )(where, freq, nodes, cen)


def main_kernel(
    where_ref, field_ref, cos_ref, sin_ref, interp_ref, eval_ref, out_ref, low_ref, high_ref, s_ref
):
    half = where_ref[1]
    nt = (((1,), (1,)), ((), ()))

    def dot(a, b):
        return lax.dot_general(a, b, nt, preferred_element_type=F32)

    def rotated(index, here, re, im):
        c, s = cos_ref[index, here, :], sin_ref[index, here, :]
        return c * re - s * im, s * re + c * im

    for level in range(3):
        for q in range(8):
            here = slice(q * 16, q * 16 + 16)
            for kind, w_ref in enumerate((low_ref, high_ref)):
                src = (q & ~(1 << level)) | (kind << level)
                there = slice(src * 16, src * 16 + 16)
                if level == 0:
                    re = field_ref[there, :K].astype(F32)
                    im = field_ref[there, K:].astype(F32)
                else:
                    re = s_ref[src * 16 : src * 16 + 16, :]
                    im = s_ref[COLS + src * 16 : COLS + src * 16 + 16, :]
                re, im = rotated(2 * level + kind, here, re, im)
                w_ref[q * 16 : q * 16 + 16, :] = re.astype(BF16)
                w_ref[COLS + q * 16 : COLS + q * 16 + 16, :] = im.astype(BF16)
        s_ref[...] = dot(low_ref[...], interp_ref[0]) + dot(high_ref[...], interp_ref[1])

    for t, w_ref in enumerate((low_ref, high_ref)):
        for q in range(8):
            here = slice(q * 16, q * 16 + 16)
            re, im = rotated(6 + t, here, s_ref[here, :], s_ref[COLS + q * 16 : COLS + q * 16 + 16, :])
            w_ref[q * 16 : q * 16 + 16, :] = re.astype(BF16)
            w_ref[COLS + q * 16 : COLS + q * 16 + 16, :] = im.astype(BF16)

    a = lax.broadcasted_iota(jnp.int32, (32, COLS), 0)
    b = lax.broadcasted_iota(jnp.int32, (32, COLS), 1)
    gather = jnp.where((a // 4 == b // 16) & (a % 4 == b % 4), 1.0, 0.0).astype(BF16)
    mine = interp_ref[half]
    for t, w_ref in enumerate((low_ref, high_ref)):
        s_ref[...] = dot(w_ref[...], mine)
        for q in range(8):
            here = slice(q * 16, q * 16 + 16)
            c, s = cos_ref[8 + t, here, :], sin_ref[8 + t, here, :]
            v = c * s_ref[here, :] - s * s_ref[COLS + q * 16 : COLS + q * 16 + 16, :]
            w_ref[here, :] = v.astype(BF16)
        v = jnp.dot(gather, w_ref[:COLS, :], preferred_element_type=F32).astype(BF16)
        out_ref[t * 32 : t * 32 + 32, :] = dot(v, eval_ref[...]).astype(BF16)


def levels(where, field, cosine, sine, interp, evaluate):
    vmem = pl.BlockSpec(memory_space=pltpu.VMEM)
    return pl.pallas_call(
        main_kernel,
        out_shape=jax.ShapeDtypeStruct((64, PIX), BF16),
        in_specs=[pl.BlockSpec(memory_space=pltpu.SMEM)] + [vmem] * 5,
        out_specs=vmem,
        scratch_shapes=[
            pltpu.VMEM((2 * COLS, K), BF16),
            pltpu.VMEM((2 * COLS, K), BF16),
            pltpu.VMEM((2 * COLS, K), F32),
        ],
        compiler_params=pltpu.CompilerParams(vmem_limit_bytes=32 * 2**20),
        cost_estimate=pl.CostEstimate(
            flops=8 * 2 * K * K * 256, bytes_accessed=10 * 2**20, transcendentals=0
        ),
        name="levels",
    )(where, field, cosine, sine, interp, evaluate)


def exchange(block, axes):
    return lax.all_to_all(block, axes, split_axis=0, concat_axis=0, tiled=True)


def body(coeffs, freqs, nodes, centres, interp, evaluate):
    where = jnp.stack([lax.axis_index("y"), lax.axis_index("z4")]).astype(jnp.int32)
    field = jnp.transpose(coeffs[0], (2, 1, 0)).reshape(32, 4, 2 * K)
    freq = jnp.transpose(freqs[0], (2, 0, 1)).reshape(1, 32, 4, 10)
    freq = jnp.broadcast_to(freq, (2, 32, 4, 10)).reshape(64, 1, 40)
    freq = exchange(freq, FAR).reshape(2, COLS, 10)
    field = exchange(field, NEAR).reshape(COLS, 2 * K)
    cosine, sine = trig(where, freq, nodes.reshape(24, K), centres.reshape(24, 64))
    part = levels(where, field, cosine, sine, interp, evaluate)
    part = part.reshape(16, 4, 8, 128).transpose(0, 2, 1, 3).reshape(128, 4, 128)
    part = exchange(part, ALL)
    total = jnp.sum(part.reshape(2, 8, 2, 4, 4, 128).astype(F32), axis=(0, 2))
    return total.reshape(COLS, 128).T


def solution(mesh):
    fine = Mesh(mesh.devices.reshape(SIZES), AXES)
    box, ang = ("y", "z4", "z2", "z1", "c"), ("zh", "x")
    return jax.shard_map(
        body,
        mesh=fine,
        in_specs=(P(ang, None, None, box), P(ang, None, None, box), P(), P(), P(), P()),
        out_specs=P(ang, box),
        check_vma=False,
    )
```

time: 250 us -> 87.3 us (0.35)
  waiting for transfers between devices: 154 us -> 9.45 us
  other arithmetic: 40.1 us -> 0.24 us
  blocking collectives: 0 us -> 28.1 us
  between operations: 13.9 us -> 0.17 us
  Pallas kernels: 0 us -> 12.8 us
  matrix products: 9.03 us -> 0 us
  starting transfers between devices: 16.5 us -> 21.5 us
    reduce_scatter x1 -> x0, waiting for transfers between devices: 111 us -> none  [body(): lax.psum_scatter(jnp.dot(evaluate, values, preferred_element_type=jnp.flo...]
    ppermute x4 -> x0, waiting for transfers between devices: 43.5 us -> none  [from_partner(): return lax.ppermute(block, axis, route)]
    all_to_all x0 -> x1, blocking collectives: none -> 28.1 us  [exchange(): return lax.all_to_all(block, axes, split_axis=0, concat_axis=0, tiled=True)]
    all_to_all x0 -> x2, starting transfers between devices: none -> 21.5 us  [exchange(): return lax.all_to_all(block, axes, split_axis=0, concat_axis=0, tiled=True)]
    add x3 -> x0, other arithmetic: 19.9 us -> none  [the longest x2 12.7 us: angle(): first = (rel_two[0][:, None] + cen_two[0][None, :]) * freq_two[0][None, :]]
    another operation x10 -> x1, other arithmetic: 17.7 us -> 0.08 us  [body(): jnp.stack([lax.axis_index('y'), lax.axis_index('z4')]).astype(jnp.int32)]
    ppermute x4 -> x0, starting transfers between devices: 16.5 us -> none  [from_partner(): return lax.ppermute(block, axis, route)]
    pallas_call x0 -> x2, Pallas kernels: none -> 12.8 us  [the longest x1 7.87 us: trig(): pl.pallas_call(trig_kernel, out_shape=[jax.ShapeDtypeStruct((10, COLS, K)...]
  transfers between devices with their start and end apart: 5 -> 2, of which waited for: 4 -> 1; matrix products, arithmetic and copies ran while one was open for 11% -> 5% of each run, Pallas kernels for 0% -> 9%
where the time goes in v1:
time: 87.3 us; the launch traced here: 86.9 us
  blocking collectives  28.1 us (32%)
  starting transfers between devices  21.5 us (25%)
  local copies, waits for them, and re-layouts  14.6 us (17%)
  Pallas kernels  12.8 us (15%)
  waiting for transfers between devices  9.45 us (11%)
    all_to_all x1, blocking collectives, exchange(): return lax.all_to_all(block, axes, split_axis=0, concat_axis=0, tiled=True)  28.1 us
    all_to_all x2, starting transfers between devices, exchange(): return lax.all_to_all(block, axes, split_axis=0, concat_axis=0, tiled=True)  21.5 us
    all_to_all x2, waiting for transfers between devices, exchange(): return lax.all_to_all(block, axes, split_axis=0, concat_axis=0, tiled=True)  9.45 us
    unnamed x16, local copies, waits for them, and re-layouts  9.09 us
    pallas_call x1, Pallas kernels, trig(): pl.pallas_call(trig_kernel, out_shape=[jax.ShapeDtypeStruct((10, COLS, K)...  7.87 us
    pallas_call x1, Pallas kernels, levels(): pl.pallas_call(main_kernel, out_shape=jax.ShapeDtypeStruct((64, PIX), BF1...  4.94 us
  transfers between devices with their start and end apart: 2, of which 1 were waited for; matrix products, arithmetic and copies ran while one was open for 5% of the time, Pallas kernels for 9%

profile of v1, /device:TPU:1, one launch (start us, length us, event | category | flops | bytes accessed | tf_op | source)
XLA Modules:
  0.0 86.9 jit_solution(6215717695364100145)
XLA Ops:
  0.0 0.0 copy-start.6
  0.0 0.9 %broadcast_in_dim.7 = bf16[32,4,10]{1,0,2:T(8,128)(2,1)S(1)} reshape(bf16[128,5,2]{0,2,1:T(2,128)(2,1)} %bitcast.33) | data formatting | bytes 5120 | tf_op jit(solution)/shard_map/broadcast_in_dim | solution.py:212
  0.9 0.2 copy.16
  1.1 0.1 reshape.34
  1.2 0.7 copy.17
  1.9 17.0 %all-to-all-start.1 = ((bf16[64,1,40]{2,1,0:T(2,128)(2,1)}), bf16[64,1,40]{2,1,0:T(2,128)(2,1)S(1)}, u32[]{:S(2)}, u32[]{:S(2)}) async-start(bf16[64,1,40]{2,1,0:T(2,128)(2,1)} %copy.17), calls=%async_computation.1 | async-start | bytes 65536 | tf_op jit(solution)/shard_map/all_to_all | solution.py:205
  19.0 1.5 %copy.15 = bf16[128,2,576]{2,1,0:T(2,128)(2,1)S(1)} copy(bf16[128,2,576]{0,1,2:T(2,128)(2,1)} %bitcast.31) | data formatting | bytes 589824 | tf_op jit(solution)/shard_map/transpose | solution.py:210
  20.5 1.0 %reshape.32 = bf16[32,4,1152]{2,1,0:T(4,128)(2,1)} reshape(bf16[128,2,576]{2,1,0:T(2,128)(2,1)S(1)} %copy.15) | data formatting | bytes 589824 | tf_op jit(solution)/shard_map/reshape | solution.py:210
  21.5 9.4 %all-to-all-done.1 = bf16[64,1,40]{2,1,0:T(2,128)(2,1)S(1)} async-done(((bf16[64,1,40]{2,1,0:T(2,128)(2,1)}), bf16[64,1,40]{2,1,0:T(2,128)(2,1)S(1)}, u32[]{:S(2)}, u32[]{:S(2)}) %all-to-all-start.1) | async-done | bytes 5152 | tf_op jit(solution)/shard_map/all_to_all | solution.py:205
  30.9 4.5 %all-to-all-start = ((bf16[32,4,1152]{2,1,0:T(4,128)(2,1)}), bf16[32,4,1152]{2,1,0:T(4,128)(2,1)S(1)}, u32[]{:S(2)}, u32[]{:S(2)}) async-start(bf16[32,4,1152]{2,1,0:T(4,128)(2,1)} %reshape.32), calls=%async_computation | async-start | bytes 589824 | tf_op jit(solution)/shard_map/all_to_all | solution.py:205
  35.4 0.0 copy-start.5
  35.5 0.0 copy-done.6
  35.5 0.0 copy-start.4
  35.5 1.8 %copy.18.eval_ref = bf16[1024,576]{1,0:T(8,128)(2,1)S(1)} copy(bf16[1024,576]{0,1:T(8,128)(2,1)} %param.11) | data formatting | bytes 2359296 | tf_op args[5]
  37.3 0.1 pad_add_fusion.where_ref
  37.4 0.1 reduce
  37.5 0.1 reshape.35.freq_ref
  37.6 0.0 copy-done.5
  37.6 7.9 %trig.1 = (f32[10,128,576]{2,1,0:T(8,128)S(1)}, f32[10,128,576]{2,1,0:T(8,128)S(1)}) custom-call(s32[2]{0:T(128)S(1)} %pad_add_fusion.where_ref, bf16[2,128,10]{2,1,0:T(8,128)(2,1)S(1)} %reshape.35.freq_ref, f32[24,576]{1,0:T(8,128)S(1)} %reshape.36.nodes_ref, f32[24,64]{1,0:T(8,128)S(1)} %bitcast.27), custom_call_target="tpu_custom_call" | custom-call | flops 29491200 | bytes 5898240 | tf_op jit(solution)/shard_map/trig/pallas_call | solution.py:119
  45.5 0.0 copy-start
  45.5 1.7 %copy-done = f32[10,128,576]{2,1,0:T(8,128)} copy-done((f32[10,128,576]{2,1,0:T(8,128)}, f32[10,128,576]{2,1,0:T(8,128)S(1)}, u32[]{:S(2)}) %copy-start) | copy-done | bytes 2949144
  47.2 0.0 copy-start.2
  47.2 1.7 %copy-done.2 = f32[10,128,576]{2,1,0:T(8,128)} copy-done((f32[10,128,576]{2,1,0:T(8,128)}, f32[10,128,576]{2,1,0:T(8,128)S(1)}, u32[]{:S(2)}) %copy-start.2) | copy-done | bytes 2949144
  48.9 0.0 all-to-all-done
  48.9 0.1 reshape.33.field_ref
  49.0 0.0 copy-done.4
  49.0 0.0 copy-start.1
  49.0 1.9 %copy-done.1 = f32[10,128,576]{2,1,0:T(8,128)S(1)} copy-done((f32[10,128,576]{2,1,0:T(8,128)S(1)}, f32[10,128,576]{2,1,0:T(8,128)}, u32[]{:S(2)}) %copy-start.1) | copy-done | bytes 2949144
  50.9 0.0 copy-start.3
  50.9 1.9 %copy-done.3 = f32[10,128,576]{2,1,0:T(8,128)S(1)} copy-done((f32[10,128,576]{2,1,0:T(8,128)S(1)}, f32[10,128,576]{2,1,0:T(8,128)}, u32[]{:S(2)}) %copy-start.3) | copy-done | bytes 2949144
  52.8 4.9 %levels.1 = bf16[64,1024]{1,0:T(8,128)(2,1)S(1)} custom-call(s32[2]{0:T(128)S(1)} %pad_add_fusion.where_ref, bf16[128,1152]{1,0:T(8,128)(2,1)S(1)} %reshape.33.field_ref, f32[10,128,576]{2,1,0:T(8,128)S(1)} %copy-done.1, f32[10,128,576]{2,1,0:T(8,128)S(1)} %copy-done.3, bf16[2,576,576]{2,1,0:T(8,128)(2,1)S(1)} %copy-done.4, bf16[1024,576]{1,0:T(8,128)(2,1)S(1)} %copy.18.eval_ref), custom_call_target="tpu_custom_call" | custom-call | flops 1358954496 | bytes 10485760 | tf_op jit(solution)/shard_map/levels/pallas_call | solution.py:186
  57.8 0.1 copy.25
  57.9 0.1 copy.20
  58.0 28.1 %all_to_all.15 = bf16[128,4,128]{2,1,0:T(4,128)(2,1)S(1)} all-to-all(bf16[128,4,128]{2,1,0:T(4,128)(2,1)S(1)} %copy.20), channel_id=1, replica_groups=mesh['y'=4,'z4'=2,'z2'=2,'z1'=2,'c'=2,'zh'=2,'x'=4] {'z4','z2','z1','c',..., dimensions={0} | all-to-all | bytes 262144 | tf_op jit(solution)/shard_map/all_to_all | solution.py:205
  86.1 0.1 convert_reduce_fusion
  86.2 0.7 copy.23
  (3 shorter events, 0.1 us)
Async XLA Ops:
  0.0 35.5 %copy-start.6 = (f32[4,3,2,576]{3,2,1,0:T(2,128)S(1)}, f32[4,3,2,576]{3,2,1,0:T(2,128)}, u32[]{:S(2)}) copy-start(f32[4,3,2,576]{3,2,1,0:T(2,128)} %param.8) | copy-start | bytes 165892
  1.9 29.0 %all-to-all-start.1 = ((bf16[64,1,40]{2,1,0:T(2,128)(2,1)}), bf16[64,1,40]{2,1,0:T(2,128)(2,1)S(1)}, u32[]{:S(2)}, u32[]{:S(2)}) async-start(bf16[64,1,40]{2,1,0:T(2,128)(2,1)} %copy.17), calls=%async_computation.1 | async-start | bytes 65536 | tf_op jit(solution)/shard_map/all_to_all | solution.py:205
  30.9 17.9 %all-to-all-start = ((bf16[32,4,1152]{2,1,0:T(4,128)(2,1)}), bf16[32,4,1152]{2,1,0:T(4,128)(2,1)S(1)}, u32[]{:S(2)}, u32[]{:S(2)}) async-start(bf16[32,4,1152]{2,1,0:T(4,128)(2,1)} %reshape.32), calls=%async_computation | async-start | bytes 589824 | tf_op jit(solution)/shard_map/all_to_all | solution.py:205
  35.4 2.2 %copy-start.5 = (f32[4,3,2,64]{3,2,1,0:T(2,128)S(1)}, f32[4,3,2,64]{3,2,1,0:T(2,128)}, u32[]{:S(2)}) copy-start(f32[4,3,2,64]{3,2,1,0:T(2,128)} %param.9) | copy-start | bytes 18436
  35.5 13.5 %copy-start.4 = (bf16[2,576,576]{2,1,0:T(8,128)(2,1)S(1)}, bf16[2,576,576]{2,1,0:T(8,128)(2,1)}, u32[]{:S(2)}) copy-start(bf16[2,576,576]{2,1,0:T(8,128)(2,1)} %interp_ref.1) | copy-start | bytes 3981316
  45.5 1.7 %copy-start = (f32[10,128,576]{2,1,0:T(8,128)}, f32[10,128,576]{2,1,0:T(8,128)S(1)}, u32[]{:S(2)}) copy-start(f32[10,128,576]{2,1,0:T(8,128)S(1)} %get-tuple-element.7.cos_ref) | copy-start | bytes 8847364
  47.2 1.7 %copy-start.2 = (f32[10,128,576]{2,1,0:T(8,128)}, f32[10,128,576]{2,1,0:T(8,128)S(1)}, u32[]{:S(2)}) copy-start(f32[10,128,576]{2,1,0:T(8,128)S(1)} %get-tuple-element.8.sin_ref) | copy-start | bytes 8847364
  49.0 1.9 %copy-start.1 = (f32[10,128,576]{2,1,0:T(8,128)S(1)}, f32[10,128,576]{2,1,0:T(8,128)}, u32[]{:S(2)}) copy-start(f32[10,128,576]{2,1,0:T(8,128)} %copy-done) | copy-start | bytes 8847364
  50.9 1.9 %copy-start.3 = (f32[10,128,576]{2,1,0:T(8,128)S(1)}, f32[10,128,576]{2,1,0:T(8,128)}, u32[]{:S(2)}) copy-start(f32[10,128,576]{2,1,0:T(8,128)} %copy-done.2) | copy-start | bytes 8847364

commit v2 on v1

v2 whole, which is shorter than its diff:
```python
import jax
import jax.numpy as jnp
import numpy as np
from jax import lax
from jax.experimental import pallas as pl
from jax.experimental.pallas import tpu as pltpu
from jax.sharding import Mesh, PartitionSpec as P

AXES = ("y", "z4", "z2", "z1", "c", "zh", "x")
SIZES = (4, 2, 2, 2, 2, 2, 4)
NEAR = ("z2", "z1", "c", "x")
ALL = ("z4", "z2", "z1", "c", "zh", "x")
K = 576
WIDE = 1280
COLS = 128
PIX = 1024
F32 = jnp.float32
BF16 = jnp.bfloat16
HIGHEST = lax.Precision.HIGHEST
VMEM = pl.BlockSpec(memory_space=pltpu.VMEM)
HBM = pl.BlockSpec(memory_space=pltpu.HBM)

COS = (
    0.999999989059023,
    -19.739204499453944,
    64.9391174598965,
    -85.45013953089278,
    60.16763095097771,
    -25.96759924841038,
    6.5286581610231424,
)
SIN = (
    6.283184916495431,
    -41.34158923268858,
    81.59994332978287,
    -76.61447253124996,
    41.34288235456833,
    -12.471243535026977,
)

OWN, LOW1, HIGH1, LOW2, HIGH2, ACROSS = range(6)
FREQS = []


def lanes_of(rows, level):
    FREQS.extend((rows, level, d) for d in range(2))
    return len(FREQS) - 2


F0, F1, F2, F3, F4 = (lanes_of(OWN, level) for level in range(5))
UP1 = lanes_of(LOW1, 0), lanes_of(HIGH1, 0)
UP2 = lanes_of(LOW2, 1), lanes_of(HIGH2, 1)
A3, A4 = (lanes_of(ACROSS, level) for level in (3, 4))

SETS = [
    [(-1, F0, 0, 0)],
    [(-1, F0, 0, 1)],
    [(1, UP1[0], 0, 2), (-1, F1, 1, 0)],
    [(1, UP1[1], 0, 2), (-1, F1, 1, 1)],
    [(1, UP2[0], 1, 2), (-1, F2, 2, 0)],
    [(1, UP2[1], 1, 2), (-1, F2, 2, 1)],
    [(1, F2, 2, 2), (-1, F3, 3, None)],
    [(1, F3, 3, 2), (1, F4, 3, 2)],
    [(1, F2, 2, 2), (-1, A3, 3, None)],
    [(1, A3, 3, 2), (1, A4, 3, 2)],
]
HERE = 8
TERMS = [
    (s, sign, lane + d, level, kind, d)
    for s, terms in enumerate(SETS)
    for sign, lane, level, kind in terms
    for d in range(2)
]


def tables():
    pick = np.zeros((6, 16, 256), np.float32)
    for lane, (rows, level, d) in enumerate(FREQS):
        at = level * 2 + d
        for piece in range(3):
            pick[rows, at, 32 * piece + lane] = 1
        for i, term in enumerate(TERMS):
            if term[2] == lane:
                pick[rows, at, 128 + i] = 1
    centre = np.zeros((2, 24, 128), np.float32)
    mask = np.zeros((8, 128), np.float32)
    for i, (s, sign, lane, level, kind, d) in enumerate(TERMS):
        for half in range(2):
            k = half if kind is None else kind
            centre[half, (level * 3 + k) * 2 + d, i] = sign
        mask[FREQS[lane][0], i] = 1
    return pick, centre, mask


PICK, CENTRE, MASK = tables()


def moved(q, rows):
    return {OWN: q, LOW1: q & ~2, HIGH1: q | 2, LOW2: q & ~4, HIGH2: q | 4}[rows]


def prepare_kernel(
    nodes_ref, cen_ref, centre_ref, mask_ref, pick_ref, b_ref, c_ref, pick_out_ref, wide_ref
):
    pick_out_ref[...] = pick_ref[...]
    base = lax.axis_index("y") * 16
    half = lax.axis_index("z4")
    turn = 0.5 / np.pi
    wide_ref[...] = jnp.zeros_like(wide_ref)
    for s, sign, lane, level, kind, d in TERMS:

        def row(kind):
            i = (level * 3 + kind) * 2 + d
            return nodes_ref[i : i + 1, :]

        value = jnp.where(half == 0, row(0), row(1)) if kind is None else row(kind)
        wide_ref[s, lane : lane + 1, :] = value * (sign * turn)
    for s in range(len(SETS)):
        rest = wide_ref[s]
        for piece in range(3):
            part = rest.astype(BF16)
            b_ref[s, 32 * piece : 32 * piece + 32, :] = part
            rest = rest - part.astype(F32)
        b_ref[s, 96:128, :] = jnp.zeros((32, K), BF16)

    picked = lax.dot_general(
        cen_ref[...] * turn,
        centre_ref[half],
        (((0,), (0,)), ((), ())),
        precision=HIGHEST,
        preferred_element_type=F32,
    )
    q = lax.broadcasted_iota(jnp.int32, (COLS, 64), 0) // 16
    lane = lax.broadcasted_iota(jnp.int32, (COLS, 64), 1)
    own = base + half * 8
    across = base + 8 - half * 8
    boxes = [own + q, own + (q & ~2), own + (q | 2), own + (q & ~4), own + (q | 4), across + q]
    total = jnp.zeros((COLS, 128), F32)
    for v, box in enumerate(boxes):
        hot = jnp.where(lane == box, 1.0, 0.0).astype(F32)
        mine = jnp.dot(hot, picked, precision=HIGHEST, preferred_element_type=F32)
        total = total + mine * mask_ref[v : v + 1, :]
    c_ref[...] = total


def prepare(nodes, cen):
    return pl.pallas_call(
        prepare_kernel,
        out_shape=[
            jax.ShapeDtypeStruct((10, 128, K), BF16),
            jax.ShapeDtypeStruct((COLS, 128), F32),
            jax.ShapeDtypeStruct(PICK.shape, BF16),
        ],
        in_specs=[VMEM] * 5,
        out_specs=[VMEM] * 3,
        scratch_shapes=[pltpu.VMEM((10, 32, K), F32)],
        compiler_params=pltpu.CompilerParams(vmem_limit_bytes=6 * 2**20),
        cost_estimate=pl.CostEstimate(flops=10**7, bytes_accessed=5 * 2**20, transcendentals=0),
        name="prepare",
    )(nodes, cen, jnp.asarray(CENTRE), jnp.asarray(MASK), jnp.asarray(PICK, BF16))


def pack_kernel(coeffs_ref, freqs_ref, out_ref):
    def spread(rows):
        i = lax.broadcasted_iota(jnp.int32, (rows, rows), 0)
        j = lax.broadcasted_iota(jnp.int32, (rows, rows), 1)
        half = rows // 2
        return jnp.where(i == 2 * (j % half) + j // half, 1.0, 0.0).astype(BF16)

    def turned(x, y):
        z = lax.dot_general(x, y, (((0,), (0,)), ((), ())), preferred_element_type=F32)
        return z.reshape(32, 4, z.shape[1]).astype(BF16)

    whole, tail = spread(256), spread(128)
    for m in range(4):
        z = turned(coeffs_ref[m * 256 : m * 256 + 256, :], whole)
        out_ref[:, :, m * 128 : m * 128 + 128] = z[:, :, :128]
        out_ref[:, :, 512 + m * 128 : 512 + m * 128 + 128] = z[:, :, 128:]
    out_ref[:, :, 1024:1152] = turned(coeffs_ref[1024:1152, :], tail)
    i = lax.broadcasted_iota(jnp.int32, (10, 128), 0)
    j = lax.broadcasted_iota(jnp.int32, (10, 128), 1)
    out_ref[:, :, 1152:] = turned(freqs_ref[...], jnp.where(i == j, 1.0, 0.0).astype(BF16))


def pack(coeffs, freqs):
    return pl.pallas_call(
        pack_kernel,
        out_shape=jax.ShapeDtypeStruct((32, 4, WIDE), BF16),
        in_specs=[VMEM] * 2,
        out_specs=VMEM,
        compiler_params=pltpu.CompilerParams(vmem_limit_bytes=4 * 2**20),
        cost_estimate=pl.CostEstimate(flops=10**7, bytes_accessed=2**20, transcendentals=0),
        name="pack",
    )(coeffs, freqs)


def horner(coefficients, u):
    total = u * coefficients[-1] + coefficients[-2]
    for value in coefficients[-3::-1]:
        total = total * u + value
    return total


def cos_sin(turns):
    r = turns - jnp.floor(turns + 0.5)
    u = r * r
    return horner(COS, u), r * horner(SIN, u)


def dot(a, b):
    return lax.dot_general(a, b, (((1,), (1,)), ((), ())), preferred_element_type=F32)


def block(q):
    return slice(q * 16, q * 16 + 16)


def phases(placed, b_ref, c_ref, sets, t_ref):
    lanes = placed[:, :128].astype(BF16)
    i = lax.broadcasted_iota(jnp.int32, (128, 128), 0)
    j = lax.broadcasted_iota(jnp.int32, (128, 128), 1)
    first = jnp.where(i < 4, i // 2, (i - 4) // 4 + 2)
    gather = jnp.where((first == j) & (i < len(TERMS)), 1.0, 0.0).astype(F32)
    const = jnp.dot(placed[:, 128:] * c_ref[...], gather, precision=HIGHEST, preferred_element_type=F32)
    for i, s in enumerate(sets):
        t_ref[i] = jnp.dot(lanes, b_ref[s], preferred_element_type=F32) + const[:, s : s + 1]


def rotated(turns, re, im):
    c, s = cos_sin(turns)
    return c * re - s * im, s * re + c * im


def contribution(state_ref, turns_ref, first, mine, fetch, evaluate_ref, w_ref, s_ref):
    for q in range(8):
        here = block(q)
        re, im = rotated(turns_ref[first, here, :], state_ref[here, :], state_ref[block(q + 8), :])
        w_ref[here, :] = re.astype(BF16)
        w_ref[block(q + 8), :] = im.astype(BF16)
    s_ref[...] = dot(w_ref[...], mine)
    for q in range(8):
        here = block(q)
        c, s = cos_sin(turns_ref[first + 1, here, :])
        v = c * s_ref[here, :] - s * s_ref[block(q + 8), :]
        w_ref[here, :] = v.astype(BF16)
    a = lax.broadcasted_iota(jnp.int32, (32, COLS), 0)
    b = lax.broadcasted_iota(jnp.int32, (32, COLS), 1)
    angles = jnp.where((a // 4 == b // 16) & (a % 4 == b % 4), 1.0, 0.0).astype(BF16)
    v = jnp.dot(angles, w_ref[:COLS, :], preferred_element_type=F32).astype(BF16)
    fetch.wait()
    return jnp.dot(v, evaluate_ref[...], preferred_element_type=F32).astype(BF16)


def fields(field_ref, q):
    x = field_ref[4 * q : 4 * q + 4].astype(F32).reshape(16, WIDE)
    re = jnp.concatenate([x[:, :512], x[:, 1024:1088]], axis=1)
    im = jnp.concatenate([x[:, 512:1024], x[:, 1088:1152]], axis=1)
    return re, im


def own_kernel(
    field_ref,
    freq_ref,
    b_ref,
    c_ref,
    pick_ref,
    interp_ref,
    eval_ref,
    out_ref,
    s_ref,
    low_ref,
    high_ref,
    last_ref,
    t_ref,
    evaluate_ref,
    sem,
):
    fetch = pltpu.make_async_copy(eval_ref, evaluate_ref, sem)
    fetch.start()
    freq = freq_ref[...].astype(F32).reshape(COLS, 128)[:, :16].astype(BF16)
    placed = jnp.zeros((COLS, 256), F32)
    for rows in range(ACROSS):
        source = jnp.concatenate([freq[block(moved(q, rows))] for q in range(8)], axis=0)
        placed = placed + jnp.dot(source, pick_ref[rows], preferred_element_type=F32)
    phases(placed, b_ref, c_ref, range(HERE), t_ref)

    for level in range(3):
        for q in range(8):
            here = block(q)
            for kind, w_ref in enumerate((low_ref, high_ref)):
                src = (q & ~(1 << level)) | (kind << level)
                if level == 0:
                    re, im = fields(field_ref, src)
                else:
                    re = s_ref[block(src), :]
                    im = s_ref[block(src + 8), :]
                re, im = rotated(t_ref[2 * level + kind, here, :], re, im)
                w_ref[here, :] = re.astype(BF16)
                w_ref[block(q + 8), :] = im.astype(BF16)
        s_ref[...] = dot(low_ref[...], interp_ref[0]) + dot(high_ref[...], interp_ref[1])
    mine = interp_ref[lax.axis_index("z4")]
    out_ref[...] = contribution(s_ref, t_ref, 6, mine, fetch, evaluate_ref, low_ref, last_ref)


def across_kernel(
    freq_ref,
    freq_across_ref,
    own_ref,
    s_ref,
    b_ref,
    c_ref,
    pick_ref,
    interp_ref,
    eval_ref,
    out_ref,
    w_ref,
    last_ref,
    t_ref,
    evaluate_ref,
    sem,
):
    fetch = pltpu.make_async_copy(eval_ref, evaluate_ref, sem)
    fetch.start()
    half = lax.axis_index("z4")
    placed = jnp.zeros((COLS, 256), F32)
    for rows, ref in ((OWN, freq_ref), (ACROSS, freq_across_ref)):
        freq = ref[...].astype(F32).reshape(COLS, 128)[:, :16].astype(BF16)
        placed = placed + jnp.dot(freq, pick_ref[rows], preferred_element_type=F32)
    phases(placed, b_ref, c_ref, (HERE, HERE + 1), t_ref)
    part = contribution(s_ref, t_ref, 0, interp_ref[half], fetch, evaluate_ref, w_ref, last_ref)
    out_ref[half] = own_ref[...]
    out_ref[1 - half] = part


def own_levels(field, freq, tables, interp, evaluate):
    return pl.pallas_call(
        own_kernel,
        out_shape=[
            jax.ShapeDtypeStruct((32, PIX), BF16),
            jax.ShapeDtypeStruct((2 * COLS, K), F32),
        ],
        in_specs=[VMEM] * 6 + [HBM],
        out_specs=[VMEM] * 2,
        scratch_shapes=[
            pltpu.VMEM((2 * COLS, K), BF16),
            pltpu.VMEM((2 * COLS, K), BF16),
            pltpu.VMEM((2 * COLS, K), F32),
            pltpu.VMEM((HERE, COLS, K), F32),
            pltpu.VMEM((K, PIX), BF16),
            pltpu.SemaphoreType.DMA,
        ],
        compiler_params=pltpu.CompilerParams(vmem_limit_bytes=12 * 2**20),
        cost_estimate=pl.CostEstimate(
            flops=8 * 2 * K * K * 256, bytes_accessed=10 * 2**20, transcendentals=0
        ),
        name="own_levels",
    )(field, freq, *tables, interp, evaluate)


def across_level(freq, freq_across, own, state, tables, interp, evaluate):
    return pl.pallas_call(
        across_kernel,
        out_shape=jax.ShapeDtypeStruct((2, 32, PIX), BF16),
        in_specs=[VMEM] * 8 + [HBM],
        out_specs=VMEM,
        scratch_shapes=[
            pltpu.VMEM((2 * COLS, K), BF16),
            pltpu.VMEM((2 * COLS, K), F32),
            pltpu.VMEM((2, COLS, K), F32),
            pltpu.VMEM((K, PIX), BF16),
            pltpu.SemaphoreType.DMA,
        ],
        compiler_params=pltpu.CompilerParams(vmem_limit_bytes=12 * 2**20),
        cost_estimate=pl.CostEstimate(
            flops=2 * 2 * K * K * 256, bytes_accessed=5 * 2**20, transcendentals=0
        ),
        name="across_level",
    )(freq, freq_across, own, state, *tables, interp, evaluate)


def exchange(block, axes):
    return lax.all_to_all(block, axes, split_axis=0, concat_axis=0, tiled=True)


def body(coeffs, freqs, nodes, centres, interp, evaluate):
    field = exchange(pack(coeffs.reshape(2 * K, COLS), freqs.reshape(10, COLS)), NEAR)
    freq = field[:, :, WIDE - 128 :]
    freq_across = lax.ppermute(freq, "z4", [(0, 1), (1, 0)])
    tables = prepare(nodes.reshape(24, K), centres.reshape(24, 64))
    own, state = own_levels(field, freq, tables, interp, evaluate.T)
    part = across_level(freq, freq_across, own, state, tables, interp, evaluate.T)
    part = part.reshape(16, 4, 8, 128).transpose(0, 2, 1, 3).reshape(128, 4, 128)
    part = exchange(part, ALL)
    total = jnp.sum(part.reshape(2, 8, 2, 4, 4, 128).astype(F32), axis=(0, 2))
    return total.reshape(COLS, 128).T


def solution(mesh):
    fine = Mesh(mesh.devices.reshape(SIZES), AXES)
    box, ang = ("y", "z4", "z2", "z1", "c"), ("zh", "x")
    return jax.shard_map(
        body,
        mesh=fine,
        in_specs=(P(ang, None, None, box), P(ang, None, None, box), P(), P(), P(), P()),
        out_specs=P(ang, box),
        check_vma=False,
    )
```

time: 87.3 us -> 71.5 us (0.82)
  local copies, waits for them, and re-layouts: 14.6 us -> 9.2 us
  Pallas kernels: 12.8 us -> 8.96 us
  starting transfers between devices: 21.5 us -> 18.7 us
  waiting for transfers between devices: 9.45 us -> 7.22 us
  blocking collectives: 28.1 us -> 26.6 us
    all_to_all x2 -> x1, starting transfers between devices: 21.5 us -> 10.4 us  [exchange(): return lax.all_to_all(block, axes, split_axis=0, concat_axis=0, tiled=True)]
    ppermute x0 -> x1, starting transfers between devices: none -> 8.32 us  [body(): freq_across = lax.ppermute(freq, 'z4', [(0, 1), (1, 0)])]
    pallas_call x2 -> x4, Pallas kernels: 12.8 us -> 8.96 us  [the longest x1 5.14 us: own_levels(): pl.pallas_call(own_kernel, out_shape=[jax.ShapeDtypeStruct((32, PIX), BF1...]
    unnamed x16 -> x21, local copies, waits for them, and re-layouts: 9.09 us -> 6.64 us
    all_to_all x2 -> x1, waiting for transfers between devices: 9.45 us -> 7.22 us  [exchange(): return lax.all_to_all(block, axes, split_axis=0, concat_axis=0, tiled=True)]
    all_to_all x1, blocking collectives: 28.1 us -> 26.6 us  [exchange(): return lax.all_to_all(block, axes, split_axis=0, concat_axis=0, tiled=True)]
    transpose x1 -> x0, local copies, waits for them, and re-layouts: 1.51 us -> none  [body(): field = jnp.transpose(coeffs[0], (2, 1, 0)).reshape(32, 4, 2 * K)]
    broadcast_in_dim x3 -> x0, local copies, waits for them, and re-layouts: 1.08 us -> none  [body(): freq = jnp.broadcast_to(freq, (2, 32, 4, 10)).reshape(64, 1, 40)]
  transfers between devices with their start and end apart: 2 -> 2, of which waited for: 1 -> 1; matrix products, arithmetic and copies ran while one was open for 5% -> 1% of each run, Pallas kernels for 9% -> 8%
where the time goes in v2:
time: 71.5 us; the launch traced here: 70.9 us
  blocking collectives  26.6 us (37%)
  starting transfers between devices  18.7 us (26%)
  local copies, waits for them, and re-layouts  9.2 us (13%)
  Pallas kernels  8.96 us (13%)
  waiting for transfers between devices  7.22 us (10%)
    all_to_all x1, blocking collectives, exchange(): return lax.all_to_all(block, axes, split_axis=0, concat_axis=0, tiled=True)  26.6 us
    all_to_all x1, starting transfers between devices, exchange(): return lax.all_to_all(block, axes, split_axis=0, concat_axis=0, tiled=True)  10.4 us
    ppermute x1, starting transfers between devices, body(): freq_across = lax.ppermute(freq, 'z4', [(0, 1), (1, 0)])  8.32 us
    all_to_all x1, waiting for transfers between devices, exchange(): return lax.all_to_all(block, axes, split_axis=0, concat_axis=0, tiled=True)  7.22 us
    unnamed x21, local copies, waits for them, and re-layouts  6.64 us
    pallas_call x1, Pallas kernels, own_levels(): pl.pallas_call(own_kernel, out_shape=[jax.ShapeDtypeStruct((32, PIX), BF1...  5.14 us
    pallas_call x1, Pallas kernels, across_level(): pl.pallas_call(across_kernel, out_shape=jax.ShapeDtypeStruct((2, 32, PIX)...  1.94 us
  transfers between devices with their start and end apart: 2, of which 1 were waited for; matrix products, arithmetic and copies ran while one was open for 1% of the time, Pallas kernels for 8%

profile of v2, /device:TPU:1, one launch (start us, length us, event | category | flops | bytes accessed | tf_op | source)
XLA Modules:
  0.0 70.9 jit_solution(3657908952728460719)
XLA Ops:
  0.0 0.0 copy-start
  0.0 0.8 %reshape.25.freqs_ref = bf16[10,128]{1,0:T(8,128)(2,1)S(1)} reshape(bf16[1,5,2,128]{3,2,1,0:T(2,128)(2,1)} %param.10) | data formatting | bytes 5120 | tf_op jit(solution)/shard_map/reshape | solution.py:386
  0.8 0.0 copy-start.2
  0.8 1.0 %copy-done.2 = bf16[1,576,2,128]{3,2,1,0:T(2,128)(2,1)S(1)} copy-done((bf16[1,576,2,128]{3,2,1,0:T(2,128)(2,1)S(1)}, bf16[1,576,2,128]{3,2,1,0:T(2,128)(2,1)}, u32[]{:S(2)}) %copy-start.2) | copy-done | bytes 294936
  1.8 1.0 %pack.1 = bf16[32,4,1280]{2,1,0:T(4,128)(2,1)} custom-call(bf16[1152,128]{1,0:T(8,128)(2,1)S(1)} %bitcast.20, bf16[10,128]{1,0:T(8,128)(2,1)S(1)} %reshape.25.freqs_ref), custom_call_target="tpu_custom_call" | custom-call | flops 10000000 | bytes 1048576 | tf_op jit(solution)/shard_map/pack/pallas_call | solution.py:186
  2.8 10.4 %all-to-all-start = ((bf16[32,4,1280]{2,1,0:T(4,128)(2,1)}), bf16[32,4,1280]{2,1,0:T(4,128)(2,1)S(1)}, u32[]{:S(2)}, u32[]{:S(2)}) async-start(bf16[32,4,1280]{2,1,0:T(4,128)(2,1)} %pack.1), calls=%async_computation | async-start | bytes 655360 | tf_op jit(solution)/shard_map/all_to_all | solution.py:382
  13.2 0.9 %reshape.26.nodes_ref = f32[24,576]{1,0:T(8,128)S(1)} reshape(f32[4,3,2,576]{3,2,1,0:T(2,128)} %param.11) | data formatting | bytes 110592 | tf_op jit(solution)/shard_map/reshape | solution.py:389
  14.1 0.0 copy-start.6
  14.1 0.8 %copy-done.6 = bf16[6,16,256]{2,1,0:T(8,128)(2,1)S(1)} copy-done((bf16[6,16,256]{2,1,0:T(8,128)(2,1)S(1)}, bf16[6,16,256]{2,1,0:T(8,128)(2,1)}, u32[]{:S(2)}) %copy-start.6) | copy-done | bytes 49176
  14.9 0.0 copy-start.7
  14.9 0.7 %copy-done.7 = f32[2,24,128]{2,1,0:T(8,128)S(1)} copy-done((f32[2,24,128]{2,1,0:T(8,128)S(1)}, f32[2,24,128]{2,1,0:T(8,128)}, u32[]{:S(2)}) %copy-start.7) | copy-done | bytes 24600
  15.7 0.0 copy-start.8
  15.7 0.7 copy-done.8
  16.4 0.0 copy-start.9
  16.4 0.7 copy-done.9
  17.1 0.9 %prepare.1 = (bf16[10,128,576]{2,1,0:T(8,128)(2,1)S(1)}, f32[128,128]{1,0:T(8,128)S(1)}, bf16[6,16,256]{2,1,0:T(8,128)(2,1)S(1)}) custom-call(f32[24,576]{1,0:T(8,128)S(1)} %reshape.26.nodes_ref, f32[24,64]{1,0:T(8,128)S(1)} %bitcast.21, f32[2,24,128]{2,1,0:T(8,128)S(1)} %copy-done.7, f32[8,128]{1,0:T(8,128)S(1)} %copy-done.9, bf16[6,16,256]{2,1,0:T(8,128)(2,1)S(1)} %copy-done.6), custom_call_target="tpu_custom_call" | custom-call | flops 10000000 | bytes 5242880 | tf_op jit(solution)/shard_map/prepare/pallas_call | solution.py:147
  17.9 0.0 copy-start.3
  17.9 0.6 copy-done.3
  18.5 7.2 %all-to-all-done.field_ref = bf16[32,4,1280]{2,1,0:T(4,128)(2,1)S(1)} async-done(((bf16[32,4,1280]{2,1,0:T(4,128)(2,1)}), bf16[32,4,1280]{2,1,0:T(4,128)(2,1)S(1)}, u32[]{:S(2)}, u32[]{:S(2)}) %all-to-all-start) | async-done | bytes 327712 | tf_op jit(solution)/shard_map/all_to_all | solution.py:382
  25.8 8.3 %collective-permute-start = (bf16[32,4,128]{2,1,0:T(4,128)(2,1)S(1)}, bf16[32,4,128]{2,1,0:T(4,128)(2,1)S(1)}, u32[]{:S(2)}, u32[]{:S(2)}) collective-permute-start(bf16[32,4,128]{2,1,0:T(4,128)(2,1)S(1)} %slice.4.freq_ref), channel_id=1, source_target_pairs={{0,64},{64,0},{1,65},{65,1},{2,66},{66,2},{3,67},{67,3},{4,68},{68... | collective-permute-start | bytes 98312 | tf_op jit(solution)/shard_map/ppermute | solution.py:388
  34.1 0.0 copy-done
  34.1 0.0 copy-start.1
  34.1 1.3 %copy-done.1 = bf16[1024,576]{0,1:T(8,128)(2,1)S(1)} copy-done((bf16[1024,576]{0,1:T(8,128)(2,1)S(1)}, bf16[1024,576]{0,1:T(8,128)(2,1)}, u32[]{:S(2)}) %copy-start.1) | copy-done | bytes 1179672
  35.4 0.0 copy-start.4
  35.4 0.8 %copy-done.4 = f32[128,128]{1,0:T(8,128)S(1)} copy-done((f32[128,128]{1,0:T(8,128)S(1)}, f32[128,128]{1,0:T(8,128)}, u32[]{:S(2)}) %copy-start.4) | copy-done | bytes 65560
  36.2 0.0 copy-start.5
  36.2 5.1 %own_levels.1 = (bf16[32,1024]{1,0:T(8,128)(2,1)S(1)}, f32[256,576]{1,0:T(8,128)S(1)}) custom-call(bf16[32,4,1280]{2,1,0:T(4,128)(2,1)S(1)} %all-to-all-done.field_ref, bf16[32,4,128]{2,1,0:T(4,128)(2,1)S(1)} %slice.4.freq_ref, bf16[10,128,576]{2,1,0:T(8,128)(2,1)S(1)} %get-tuple-element.10.b_ref, f32[128,128]{1,0:T(8,128)S(1)} %copy-done.4, ...), custom_call_target="tpu_custom_call" | custom-call | flops 1358954496 | bytes 10485760 | tf_op jit(solution)/shard_map/own_levels/pallas_call | solution.py:336
  41.4 0.0 collective-permute-done.freq_across_ref
  41.4 0.0 copy-done.5
  41.4 1.9 %across_level.1 = bf16[2,32,1024]{2,1,0:T(8,128)(2,1)S(1)} custom-call(bf16[32,4,128]{2,1,0:T(4,128)(2,1)S(1)} %slice.4.freq_ref, bf16[32,4,128]{2,1,0:T(4,128)(2,1)S(1)} %collective-permute-done.freq_across_ref, bf16[32,1024]{1,0:T(8,128)(2,1)S(1)} %get-tuple-element.13.own_ref, f32[256,576]{1,0:T(8,128)S(1)} %get-tuple-element.14.s_ref, ...), custom_call_target="tpu_custom_call" | custom-call | flops 339738624 | bytes 5242880 | tf_op jit(solution)/shard_map/across_level/pallas_call | solution.py:361
  43.4 0.1 copy.13
  43.5 26.6 %all_to_all.10 = bf16[128,4,128]{2,1,0:T(4,128)(2,1)S(1)} all-to-all(bf16[128,4,128]{2,1,0:T(4,128)(2,1)S(1)} %copy.13), channel_id=1, replica_groups=mesh['y'=4,'z4'=2,'z2'=2,'z1'=2,'c'=2,'zh'=2,'x'=4] {'z4','z2','z1','c',..., dimensions={0} | all-to-all | bytes 262144 | tf_op jit(solution)/shard_map/all_to_all | solution.py:382
  70.1 0.1 convert_reduce_fusion
  70.2 0.7 %copy.16 = f32[128,128]{1,0:T(8,128)} copy(f32[128,128]{0,1:T(8,128)S(1)} %bitcast.25) | data formatting | bytes 131072 | tf_op jit(solution)/shard_map/transpose | solution.py:395
  (3 shorter events, 0.1 us)
Async XLA Ops:
  0.0 34.1 %copy-start = (bf16[2,576,576]{2,1,0:T(8,128)(2,1)S(1)}, bf16[2,576,576]{2,1,0:T(8,128)(2,1)}, u32[]{:S(2)}) copy-start(bf16[2,576,576]{2,1,0:T(8,128)(2,1)} %interp_ref.3) | copy-start | bytes 3981316
  0.8 1.0 %copy-start.2 = (bf16[1,576,2,128]{3,2,1,0:T(2,128)(2,1)S(1)}, bf16[1,576,2,128]{3,2,1,0:T(2,128)(2,1)}, u32[]{:S(2)}) copy-start(bf16[1,576,2,128]{3,2,1,0:T(2,128)(2,1)} %param.9) | copy-start | bytes 884740
  2.8 23.0 %all-to-all-start = ((bf16[32,4,1280]{2,1,0:T(4,128)(2,1)}), bf16[32,4,1280]{2,1,0:T(4,128)(2,1)S(1)}, u32[]{:S(2)}, u32[]{:S(2)}) async-start(bf16[32,4,1280]{2,1,0:T(4,128)(2,1)} %pack.1), calls=%async_computation | async-start | bytes 655360 | tf_op jit(solution)/shard_map/all_to_all | solution.py:382
  14.1 0.8 %copy-start.6 = (bf16[6,16,256]{2,1,0:T(8,128)(2,1)S(1)}, bf16[6,16,256]{2,1,0:T(8,128)(2,1)}, u32[]{:S(2)}) copy-start(bf16[6,16,256]{2,1,0:T(8,128)(2,1)} %constant.10.clone.pick_ref) | copy-start | bytes 147460
  14.9 0.7 %copy-start.7 = (f32[2,24,128]{2,1,0:T(8,128)S(1)}, f32[2,24,128]{2,1,0:T(8,128)}, u32[]{:S(2)}) copy-start(f32[2,24,128]{2,1,0:T(8,128)} %constant.8.clone.centre_ref) | copy-start | bytes 73732
  15.7 0.7 copy-start.8
  16.4 0.7 copy-start.9
  17.9 0.6 copy-start.3
  25.8 15.6 %collective-permute-start = (bf16[32,4,128]{2,1,0:T(4,128)(2,1)S(1)}, bf16[32,4,128]{2,1,0:T(4,128)(2,1)S(1)}, u32[]{:S(2)}, u32[]{:S(2)}) collective-permute-start(bf16[32,4,128]{2,1,0:T(4,128)(2,1)S(1)} %slice.4.freq_ref), channel_id=1, source_target_pairs={{0,64},{64,0},{1,65},{65,1},{2,66},{66,2},{3,67},{67,3},{4,68},{68... | collective-permute-start | bytes 98312 | tf_op jit(solution)/shard_map/ppermute | solution.py:388
  34.1 1.3 %copy-start.1 = (bf16[1024,576]{0,1:T(8,128)(2,1)S(1)}, bf16[1024,576]{0,1:T(8,128)(2,1)}, u32[]{:S(2)}) copy-start(bf16[1024,576]{0,1:T(8,128)(2,1)} %param.14) | copy-start | bytes 3538948
  35.4 0.8 %copy-start.4 = (f32[128,128]{1,0:T(8,128)S(1)}, f32[128,128]{1,0:T(8,128)}, u32[]{:S(2)}) copy-start(f32[128,128]{1,0:T(8,128)} %copy-done.3) | copy-start | bytes 196612
  36.2 5.2 %copy-start.5 = (f32[128,128]{1,0:T(8,128)S(1)}, f32[128,128]{1,0:T(8,128)}, u32[]{:S(2)}) copy-start(f32[128,128]{1,0:T(8,128)} %copy-done.3) | copy-start | bytes 196612

commit v3 on v2

--- a/solution.py
+++ b/solution.py
@@ -18,7 +18,6 @@
 BF16 = jnp.bfloat16
 HIGHEST = lax.Precision.HIGHEST
 VMEM = pl.BlockSpec(memory_space=pltpu.VMEM)
-HBM = pl.BlockSpec(memory_space=pltpu.HBM)
 
 COS = (
     0.999999989059023,
@@ -99,13 +98,17 @@
     return {OWN: q, LOW1: q & ~2, HIGH1: q | 2, LOW2: q & ~4, HIGH2: q | 4}[rows]
 
 
-def prepare_kernel(
-    nodes_ref, cen_ref, centre_ref, mask_ref, pick_ref, b_ref, c_ref, pick_out_ref, wide_ref
-):
-    pick_out_ref[...] = pick_ref[...]
+def prepare_kernel(nodes_ref, cen_ref, centre_ref, mask_ref, pick_ref, out_ref, wide_ref):
     base = lax.axis_index("y") * 16
     half = lax.axis_index("z4")
     turn = 0.5 / np.pi
+
+    def pieces(rest):
+        for piece in range(3):
+            part = rest.astype(BF16)
+            yield piece, part
+            rest = rest - part.astype(F32)
+
     wide_ref[...] = jnp.zeros_like(wide_ref)
     for s, sign, lane, level, kind, d in TERMS:
 
@@ -116,12 +119,8 @@
         value = jnp.where(half == 0, row(0), row(1)) if kind is None else row(kind)
         wide_ref[s, lane : lane + 1, :] = value * (sign * turn)
     for s in range(len(SETS)):
-        rest = wide_ref[s]
-        for piece in range(3):
-            part = rest.astype(BF16)
-            b_ref[s, 32 * piece : 32 * piece + 32, :] = part
-            rest = rest - part.astype(F32)
-        b_ref[s, 96:128, :] = jnp.zeros((32, K), BF16)
+        for piece, part in pieces(wide_ref[s]):
+            out_ref[s, 32 * piece : 32 * piece + 32, :] = part
 
     picked = lax.dot_general(
         cen_ref[...] * turn,
@@ -130,34 +129,32 @@
         precision=HIGHEST,
         preferred_element_type=F32,
     )
-    q = lax.broadcasted_iota(jnp.int32, (COLS, 64), 0) // 16
-    lane = lax.broadcasted_iota(jnp.int32, (COLS, 64), 1)
+    q = lax.broadcasted_iota(jnp.int32, (32, 64), 0) & 7
+    lane = lax.broadcasted_iota(jnp.int32, (32, 64), 1)
     own = base + half * 8
     across = base + 8 - half * 8
     boxes = [own + q, own + (q & ~2), own + (q | 2), own + (q & ~4), own + (q | 4), across + q]
-    total = jnp.zeros((COLS, 128), F32)
+    total = jnp.zeros((32, 128), F32)
     for v, box in enumerate(boxes):
         hot = jnp.where(lane == box, 1.0, 0.0).astype(F32)
         mine = jnp.dot(hot, picked, precision=HIGHEST, preferred_element_type=F32)
         total = total + mine * mask_ref[v : v + 1, :]
-    c_ref[...] = total
+    for piece, part in pieces(total):
+        out_ref[10, 32 * piece : 32 * piece + 32, :128] = part
+    out_ref[11, :, :256] = pick_ref[...]
 
 
 def prepare(nodes, cen):
     return pl.pallas_call(
         prepare_kernel,
-        out_shape=[
-            jax.ShapeDtypeStruct((10, 128, K), BF16),
-            jax.ShapeDtypeStruct((COLS, 128), F32),
-            jax.ShapeDtypeStruct(PICK.shape, BF16),
-        ],
+        out_shape=jax.ShapeDtypeStruct((12, 96, K), BF16),
         in_specs=[VMEM] * 5,
-        out_specs=[VMEM] * 3,
+        out_specs=VMEM,
         scratch_shapes=[pltpu.VMEM((10, 32, K), F32)],
         compiler_params=pltpu.CompilerParams(vmem_limit_bytes=6 * 2**20),
         cost_estimate=pl.CostEstimate(flops=10**7, bytes_accessed=5 * 2**20, transcendentals=0),
         name="prepare",
-    )(nodes, cen, jnp.asarray(CENTRE), jnp.asarray(MASK), jnp.asarray(PICK, BF16))
+    )(nodes, cen, jnp.asarray(CENTRE), jnp.asarray(MASK), jnp.asarray(PICK.reshape(96, 256), BF16))
 
 
 def pack_kernel(coeffs_ref, freqs_ref, out_ref):
@@ -179,7 +176,7 @@
     out_ref[:, :, 1024:1152] = turned(coeffs_ref[1024:1152, :], tail)
     i = lax.broadcasted_iota(jnp.int32, (10, 128), 0)
     j = lax.broadcasted_iota(jnp.int32, (10, 128), 1)
-    out_ref[:, :, 1152:] = turned(freqs_ref[...], jnp.where(i == j, 1.0, 0.0).astype(BF16))
+    out_ref[:, :, 1152:] = turned(freqs_ref[...].astype(F32).reshape(10, COLS).astype(BF16), jnp.where(i == j, 1.0, 0.0).astype(BF16))
 
 
 def pack(coeffs, freqs):
@@ -215,15 +212,25 @@
     return slice(q * 16, q * 16 + 16)
 
 
-def phases(placed, b_ref, c_ref, sets, t_ref):
-    lanes = placed[:, :128].astype(BF16)
+def picked(table_ref, rows, freq):
+    pick = table_ref[11, 16 * rows : 16 * rows + 16, :256]
+    return jnp.dot(freq, pick, preferred_element_type=F32)
+
+
+def phases(placed, table_ref, sets, t_ref):
+    lanes = placed[:, :96].astype(BF16)
     i = lax.broadcasted_iota(jnp.int32, (128, 128), 0)
     j = lax.broadcasted_iota(jnp.int32, (128, 128), 1)
     first = jnp.where(i < 4, i // 2, (i - 4) // 4 + 2)
     gather = jnp.where((first == j) & (i < len(TERMS)), 1.0, 0.0).astype(F32)
-    const = jnp.dot(placed[:, 128:] * c_ref[...], gather, precision=HIGHEST, preferred_element_type=F32)
+    high, mid, low = (table_ref[10, 32 * p : 32 * p + 32, :128].astype(F32) for p in range(3))
+    centre = high + mid + low
+    centre = jnp.concatenate(
+        [jnp.broadcast_to(centre[q : q + 1], (16, 128)) for q in range(8)], axis=0
+    )
+    const = jnp.dot(placed[:, 128:] * centre, gather, precision=HIGHEST, preferred_element_type=F32)
     for i, s in enumerate(sets):
-        t_ref[i] = jnp.dot(lanes, b_ref[s], preferred_element_type=F32) + const[:, s : s + 1]
+        t_ref[i] = jnp.dot(lanes, table_ref[s], preferred_element_type=F32) + const[:, s : s + 1]
 
 
 def rotated(turns, re, im):
@@ -231,7 +238,7 @@
     return c * re - s * im, s * re + c * im
 
 
-def contribution(state_ref, turns_ref, first, mine, fetch, evaluate_ref, w_ref, s_ref):
+def contribution(state_ref, turns_ref, first, mine, w_ref, s_ref):
     for q in range(8):
         here = block(q)
         re, im = rotated(turns_ref[first, here, :], state_ref[here, :], state_ref[block(q + 8), :])
@@ -246,9 +253,7 @@
     a = lax.broadcasted_iota(jnp.int32, (32, COLS), 0)
     b = lax.broadcasted_iota(jnp.int32, (32, COLS), 1)
     angles = jnp.where((a // 4 == b // 16) & (a % 4 == b % 4), 1.0, 0.0).astype(BF16)
-    v = jnp.dot(angles, w_ref[:COLS, :], preferred_element_type=F32).astype(BF16)
-    fetch.wait()
-    return jnp.dot(v, evaluate_ref[...], preferred_element_type=F32).astype(BF16)
+    return jnp.dot(angles, w_ref[:COLS, :], preferred_element_type=F32).astype(BF16)
 
 
 def fields(field_ref, q):
@@ -258,31 +263,19 @@
     return re, im
 
 
+def lanes_16(freq_ref):
+    return freq_ref[...].astype(F32).reshape(COLS, 128)[:, :16].astype(BF16)
+
+
 def own_kernel(
-    field_ref,
-    freq_ref,
-    b_ref,
-    c_ref,
-    pick_ref,
-    interp_ref,
-    eval_ref,
-    out_ref,
-    s_ref,
-    low_ref,
-    high_ref,
-    last_ref,
-    t_ref,
-    evaluate_ref,
-    sem,
+    field_ref, freq_ref, table_ref, interp_ref, v_ref, s_ref, low_ref, high_ref, last_ref, t_ref
 ):
-    fetch = pltpu.make_async_copy(eval_ref, evaluate_ref, sem)
-    fetch.start()
-    freq = freq_ref[...].astype(F32).reshape(COLS, 128)[:, :16].astype(BF16)
+    freq = lanes_16(freq_ref)
     placed = jnp.zeros((COLS, 256), F32)
     for rows in range(ACROSS):
         source = jnp.concatenate([freq[block(moved(q, rows))] for q in range(8)], axis=0)
-        placed = placed + jnp.dot(source, pick_ref[rows], preferred_element_type=F32)
-    phases(placed, b_ref, c_ref, range(HERE), t_ref)
+        placed = placed + picked(table_ref, rows, source)
+    phases(placed, table_ref, range(HERE), t_ref)
 
     for level in range(3):
         for q in range(8):
@@ -299,83 +292,72 @@
                 w_ref[block(q + 8), :] = im.astype(BF16)
         s_ref[...] = dot(low_ref[...], interp_ref[0]) + dot(high_ref[...], interp_ref[1])
     mine = interp_ref[lax.axis_index("z4")]
-    out_ref[...] = contribution(s_ref, t_ref, 6, mine, fetch, evaluate_ref, low_ref, last_ref)
+    v_ref[...] = contribution(s_ref, t_ref, 6, mine, low_ref, last_ref)
 
 
 def across_kernel(
     freq_ref,
     freq_across_ref,
-    own_ref,
+    v_ref,
     s_ref,
-    b_ref,
-    c_ref,
-    pick_ref,
+    table_ref,
     interp_ref,
     eval_ref,
     out_ref,
     w_ref,
     last_ref,
     t_ref,
-    evaluate_ref,
-    sem,
 ):
-    fetch = pltpu.make_async_copy(eval_ref, evaluate_ref, sem)
-    fetch.start()
     half = lax.axis_index("z4")
-    placed = jnp.zeros((COLS, 256), F32)
-    for rows, ref in ((OWN, freq_ref), (ACROSS, freq_across_ref)):
-        freq = ref[...].astype(F32).reshape(COLS, 128)[:, :16].astype(BF16)
-        placed = placed + jnp.dot(freq, pick_ref[rows], preferred_element_type=F32)
-    phases(placed, b_ref, c_ref, (HERE, HERE + 1), t_ref)
-    part = contribution(s_ref, t_ref, 0, interp_ref[half], fetch, evaluate_ref, w_ref, last_ref)
-    out_ref[half] = own_ref[...]
-    out_ref[1 - half] = part
-
-
-def own_levels(field, freq, tables, interp, evaluate):
+    placed = picked(table_ref, OWN, lanes_16(freq_ref))
+    placed = placed + picked(table_ref, ACROSS, lanes_16(freq_across_ref))
+    phases(placed, table_ref, (HERE, HERE + 1), t_ref)
+    v = contribution(s_ref, t_ref, 0, interp_ref[half], w_ref, last_ref)
+    for where, value in ((half, v_ref[...]), (1 - half, v)):
+        part = jnp.dot(value, eval_ref[...], preferred_element_type=F32)
+        out_ref[where] = part.astype(BF16)
+
+
+def own_levels(field, freq, table, interp):
     return pl.pallas_call(
         own_kernel,
         out_shape=[
-            jax.ShapeDtypeStruct((32, PIX), BF16),
+            jax.ShapeDtypeStruct((32, K), BF16),
             jax.ShapeDtypeStruct((2 * COLS, K), F32),
         ],
-        in_specs=[VMEM] * 6 + [HBM],
+        in_specs=[VMEM] * 4,
         out_specs=[VMEM] * 2,
         scratch_shapes=[
             pltpu.VMEM((2 * COLS, K), BF16),
             pltpu.VMEM((2 * COLS, K), BF16),
             pltpu.VMEM((2 * COLS, K), F32),
             pltpu.VMEM((HERE, COLS, K), F32),
-            pltpu.VMEM((K, PIX), BF16),
-            pltpu.SemaphoreType.DMA,
         ],
-        compiler_params=pltpu.CompilerParams(vmem_limit_bytes=12 * 2**20),
+        compiler_params=pltpu.CompilerParams(vmem_limit_bytes=8 * 2**20),
         cost_estimate=pl.CostEstimate(
             flops=8 * 2 * K * K * 256, bytes_accessed=10 * 2**20, transcendentals=0
         ),
         name="own_levels",
-    )(field, freq, *tables, interp, evaluate)
-
-
-def across_level(freq, freq_across, own, state, tables, interp, evaluate):
+    )(field, freq, table, interp)
+
+
+def across_level(freq, freq_across, v, state, table, interp, evaluate):
     return pl.pallas_call(
         across_kernel,
         out_shape=jax.ShapeDtypeStruct((2, 32, PIX), BF16),
-        in_specs=[VMEM] * 8 + [HBM],
+        in_specs=[VMEM] * 7,
         out_specs=VMEM,
         scratch_shapes=[
             pltpu.VMEM((2 * COLS, K), BF16),
             pltpu.VMEM((2 * COLS, K), F32),
             pltpu.VMEM((2, COLS, K), F32),
-            pltpu.VMEM((K, PIX), BF16),
-            pltpu.SemaphoreType.DMA,
         ],
-        compiler_params=pltpu.CompilerParams(vmem_limit_bytes=12 * 2**20),
+        compiler_params=pltpu.CompilerParams(vmem_limit_bytes=6 * 2**20),
         cost_estimate=pl.CostEstimate(
             flops=2 * 2 * K * K * 256, bytes_accessed=5 * 2**20, transcendentals=0
         ),
         name="across_level",
-    )(freq, freq_across, own, state, *tables, interp, evaluate)
+    )(freq, freq_across, v, state, table, interp, evaluate)
 
 
 def exchange(block, axes):
@@ -383,12 +365,12 @@
 
 
 def body(coeffs, freqs, nodes, centres, interp, evaluate):
-    field = exchange(pack(coeffs.reshape(2 * K, COLS), freqs.reshape(10, COLS)), NEAR)
+    field = exchange(pack(coeffs.reshape(2 * K, COLS), freqs[0]), NEAR)
     freq = field[:, :, WIDE - 128 :]
     freq_across = lax.ppermute(freq, "z4", [(0, 1), (1, 0)])
-    tables = prepare(nodes.reshape(24, K), centres.reshape(24, 64))
-    own, state = own_levels(field, freq, tables, interp, evaluate.T)
-    part = across_level(freq, freq_across, own, state, tables, interp, evaluate.T)
+    table = prepare(nodes.reshape(24, K), centres.reshape(24, 64))
+    v, state = own_levels(field, freq, table, interp)
+    part = across_level(freq, freq_across, v, state, table, interp, evaluate.T)
     part = part.reshape(16, 4, 8, 128).transpose(0, 2, 1, 3).reshape(128, 4, 128)
     part = exchange(part, ALL)
     total = jnp.sum(part.reshape(2, 8, 2, 4, 4, 128).astype(F32), axis=(0, 2))

time: 71.5 us -> 70.1 us (0.980)
  local copies, waits for them, and re-layouts: 9.2 us -> 6.36 us
  blocking collectives: 26.6 us -> 28.1 us
  Pallas kernels: 8.96 us -> 8 us
  waiting for transfers between devices: 7.22 us -> 8.09 us
    unnamed x21 -> x17, local copies, waits for them, and re-layouts: 6.64 us -> 4.61 us
    all_to_all x1, blocking collectives: 26.6 us -> 28.1 us  [exchange(): return lax.all_to_all(block, axes, split_axis=0, concat_axis=0, tiled=True)]
    all_to_all x1, waiting for transfers between devices: 7.22 us -> 8.09 us  [exchange(): return lax.all_to_all(block, axes, split_axis=0, concat_axis=0, tiled=True)]
    reshape x2 -> x1, local copies, waits for them, and re-layouts: 1.69 us -> 0.87 us  [body(): table = prepare(nodes.reshape(24, K), centres.reshape(24, 64))]
    pallas_call x2, Pallas kernels: 5.99 us -> 5.24 us  [the longest x1 4.63 us: own_levels(): pl.pallas_call(own_kernel, out_shape=[jax.ShapeDtypeStruct((32, K), BF16)...]
where the time goes in v3:
time: 70.1 us; the launch traced here: 69.6 us
  blocking collectives  28.1 us (40%)
  starting transfers between devices  18.9 us (27%)
  waiting for transfers between devices  8.09 us (12%)
  Pallas kernels  8 us (11%)
  local copies, waits for them, and re-layouts  6.36 us (9%)
    all_to_all x1, blocking collectives, exchange(): return lax.all_to_all(block, axes, split_axis=0, concat_axis=0, tiled=True)  28.1 us
    all_to_all x1, starting transfers between devices, exchange(): return lax.all_to_all(block, axes, split_axis=0, concat_axis=0, tiled=True)  10.4 us
    ppermute x1, starting transfers between devices, body(): freq_across = lax.ppermute(freq, 'z4', [(0, 1), (1, 0)])  8.45 us
    all_to_all x1, waiting for transfers between devices, exchange(): return lax.all_to_all(block, axes, split_axis=0, concat_axis=0, tiled=True)  8.09 us
    pallas_call x1, Pallas kernels, own_levels(): pl.pallas_call(own_kernel, out_shape=[jax.ShapeDtypeStruct((32, K), BF16)...  4.63 us
    unnamed x17, local copies, waits for them, and re-layouts  4.61 us
    pallas_call x1, Pallas kernels, across_level(): pl.pallas_call(across_kernel, out_shape=jax.ShapeDtypeStruct((2, 32, PIX)...  1.73 us
  transfers between devices with their start and end apart: 2, of which 1 were waited for; matrix products, arithmetic and copies ran while one was open for 1% of the time, Pallas kernels for 8%

profile of v3, /device:TPU:1, one launch (start us, length us, event | category | flops | bytes accessed | tf_op | source)
XLA Modules:
  0.0 69.6 jit_solution(16924806823021192659)
XLA Ops:
  0.0 0.0 copy-start.2
  0.0 1.0 %copy-done.2 = bf16[1,576,2,128]{3,2,1,0:T(2,128)(2,1)S(1)} copy-done((bf16[1,576,2,128]{3,2,1,0:T(2,128)(2,1)S(1)}, bf16[1,576,2,128]{3,2,1,0:T(2,128)(2,1)}, u32[]{:S(2)}) %copy-start.2) | copy-done | bytes 294936
  1.0 0.0 copy-start.7
  1.0 0.7 copy-done.7
  1.6 0.0 copy-start
  1.6 1.0 %pack.1 = bf16[32,4,1280]{2,1,0:T(4,128)(2,1)} custom-call(bf16[1152,128]{1,0:T(8,128)(2,1)S(1)} %bitcast.20, bf16[5,2,128]{2,1,0:T(2,128)(2,1)S(1)} %bitcast.22), custom_call_target="tpu_custom_call" | custom-call | flops 10000000 | bytes 1048576 | tf_op jit(solution)/shard_map/pack/pallas_call | solution.py:183
  2.7 10.4 %all-to-all-start = ((bf16[32,4,1280]{2,1,0:T(4,128)(2,1)}), bf16[32,4,1280]{2,1,0:T(4,128)(2,1)S(1)}, u32[]{:S(2)}, u32[]{:S(2)}) async-start(bf16[32,4,1280]{2,1,0:T(4,128)(2,1)} %pack.1), calls=%async_computation | async-start | bytes 655360 | tf_op jit(solution)/shard_map/all_to_all | solution.py:364
  13.1 0.9 %reshape.22.nodes_ref = f32[24,576]{1,0:T(8,128)S(1)} reshape(f32[4,3,2,576]{3,2,1,0:T(2,128)} %param.11) | data formatting | bytes 110592 | tf_op jit(solution)/shard_map/reshape | solution.py:371
  14.0 0.0 copy-start.3
  14.0 0.8 %copy-done.3 = bf16[96,256]{1,0:T(8,128)(2,1)S(1)} copy-done((bf16[96,256]{1,0:T(8,128)(2,1)S(1)}, bf16[96,256]{1,0:T(8,128)(2,1)}, u32[]{:S(2)}) %copy-start.3) | copy-done | bytes 49176
  14.8 0.0 copy-start.4
  14.8 0.7 %copy-done.4 = f32[2,24,128]{2,1,0:T(8,128)S(1)} copy-done((f32[2,24,128]{2,1,0:T(8,128)S(1)}, f32[2,24,128]{2,1,0:T(8,128)}, u32[]{:S(2)}) %copy-start.4) | copy-done | bytes 24600
  15.5 0.0 copy-start.5
  15.5 0.7 %copy-done.5 = f32[4,3,2,64]{3,2,1,0:T(2,128)S(1)} copy-done((f32[4,3,2,64]{3,2,1,0:T(2,128)S(1)}, f32[4,3,2,64]{3,2,1,0:T(2,128)}, u32[]{:S(2)}) %copy-start.5) | copy-done | bytes 6168
  16.2 0.0 copy-start.6
  16.2 0.7 copy-done.6
  16.9 0.6 prepare.1.table_ref
  17.5 8.1 %all-to-all-done.field_ref = bf16[32,4,1280]{2,1,0:T(4,128)(2,1)S(1)} async-done(((bf16[32,4,1280]{2,1,0:T(4,128)(2,1)}), bf16[32,4,1280]{2,1,0:T(4,128)(2,1)S(1)}, u32[]{:S(2)}, u32[]{:S(2)}) %all-to-all-start) | async-done | bytes 327712 | tf_op jit(solution)/shard_map/all_to_all | solution.py:364
  25.7 0.0 copy-start.1
  25.7 8.5 %collective-permute-start = (bf16[32,4,128]{2,1,0:T(4,128)(2,1)S(1)}, bf16[32,4,128]{2,1,0:T(4,128)(2,1)S(1)}, u32[]{:S(2)}, u32[]{:S(2)}) collective-permute-start(bf16[32,4,128]{2,1,0:T(4,128)(2,1)S(1)} %slice.4.freq_ref), channel_id=1, source_target_pairs={{0,64},{64,0},{1,65},{65,1},{2,66},{66,2},{3,67},{67,3},{4,68},{68... | collective-permute-start | bytes 98312 | tf_op jit(solution)/shard_map/ppermute | solution.py:370
  34.1 0.0 copy-done
  34.1 4.6 %own_levels.1 = (bf16[32,576]{1,0:T(8,128)(2,1)S(1)}, f32[256,576]{1,0:T(8,128)S(1)}) custom-call(bf16[32,4,1280]{2,1,0:T(4,128)(2,1)S(1)} %all-to-all-done.field_ref, bf16[32,4,128]{2,1,0:T(4,128)(2,1)S(1)} %slice.4.freq_ref, bf16[12,96,576]{2,1,0:T(8,128)(2,1)S(1)} %prepare.1.table_ref, bf16[2,576,576]{2,1,0:T(8,128)(2,1)S(1)} %copy-done), custom_call_target="tpu_custom_call" | custom-call | flops 1358954496 | bytes 10485760 | tf_op jit(solution)/shard_map/own_levels/pallas_call | solution.py:322
  38.8 0.0 collective-permute-done.freq_across_ref
  38.8 0.0 copy-done.1
  38.8 1.7 %across_level.1 = bf16[2,32,1024]{2,1,0:T(8,128)(2,1)S(1)} custom-call(bf16[32,4,128]{2,1,0:T(4,128)(2,1)S(1)} %slice.4.freq_ref, bf16[32,4,128]{2,1,0:T(4,128)(2,1)S(1)} %collective-permute-done.freq_across_ref, bf16[32,576]{1,0:T(8,128)(2,1)S(1)} %get-tuple-element.7.v_ref, f32[256,576]{1,0:T(8,128)S(1)} %get-tuple-element.8.s_ref, ...), custom_call_target="tpu_custom_call" | custom-call | flops 339738624 | bytes 5242880 | tf_op jit(solution)/shard_map/across_level/pallas_call | solution.py:345
  40.6 0.1 copy.13
  40.7 28.1 %all_to_all.10 = bf16[128,4,128]{2,1,0:T(4,128)(2,1)S(1)} all-to-all(bf16[128,4,128]{2,1,0:T(4,128)(2,1)S(1)} %copy.13), channel_id=1, replica_groups=mesh['y'=4,'z4'=2,'z2'=2,'z1'=2,'c'=2,'zh'=2,'x'=4] {'z4','z2','z1','c',..., dimensions={0} | all-to-all | bytes 262144 | tf_op jit(solution)/shard_map/all_to_all | solution.py:364
  68.8 0.1 convert_reduce_fusion
  68.9 0.7 %copy.16 = f32[128,128]{1,0:T(8,128)} copy(f32[128,128]{0,1:T(8,128)S(1)} %bitcast.26) | data formatting | bytes 131072 | tf_op jit(solution)/shard_map/transpose | solution.py:377
  (3 shorter events, 0.1 us)
Async XLA Ops:
  0.0 1.0 %copy-start.2 = (bf16[1,576,2,128]{3,2,1,0:T(2,128)(2,1)S(1)}, bf16[1,576,2,128]{3,2,1,0:T(2,128)(2,1)}, u32[]{:S(2)}) copy-start(bf16[1,576,2,128]{3,2,1,0:T(2,128)(2,1)} %param.9) | copy-start | bytes 884740
  1.0 0.7 copy-start.7
  1.6 32.5 %copy-start = (bf16[2,576,576]{2,1,0:T(8,128)(2,1)S(1)}, bf16[2,576,576]{2,1,0:T(8,128)(2,1)}, u32[]{:S(2)}) copy-start(bf16[2,576,576]{2,1,0:T(8,128)(2,1)} %interp_ref.3) | copy-start | bytes 3981316
  2.7 23.0 %all-to-all-start = ((bf16[32,4,1280]{2,1,0:T(4,128)(2,1)}), bf16[32,4,1280]{2,1,0:T(4,128)(2,1)S(1)}, u32[]{:S(2)}, u32[]{:S(2)}) async-start(bf16[32,4,1280]{2,1,0:T(4,128)(2,1)} %pack.1), calls=%async_computation | async-start | bytes 655360 | tf_op jit(solution)/shard_map/all_to_all | solution.py:364
  14.0 0.8 %copy-start.3 = (bf16[96,256]{1,0:T(8,128)(2,1)S(1)}, bf16[96,256]{1,0:T(8,128)(2,1)}, u32[]{:S(2)}) copy-start(bf16[96,256]{1,0:T(8,128)(2,1)} %constant.10.clone.pick_ref) | copy-start | bytes 147460
  14.8 0.7 %copy-start.4 = (f32[2,24,128]{2,1,0:T(8,128)S(1)}, f32[2,24,128]{2,1,0:T(8,128)}, u32[]{:S(2)}) copy-start(f32[2,24,128]{2,1,0:T(8,128)} %constant.8.clone.centre_ref) | copy-start | bytes 73732
  15.5 0.7 %copy-start.5 = (f32[4,3,2,64]{3,2,1,0:T(2,128)S(1)}, f32[4,3,2,64]{3,2,1,0:T(2,128)}, u32[]{:S(2)}) copy-start(f32[4,3,2,64]{3,2,1,0:T(2,128)} %param.12) | copy-start | bytes 18436
  16.2 0.7 copy-start.6
  25.7 13.1 %copy-start.1 = (bf16[1024,576]{0,1:T(8,128)(2,1)S(1)}, bf16[1024,576]{0,1:T(8,128)(2,1)}, u32[]{:S(2)}) copy-start(bf16[1024,576]{0,1:T(8,128)(2,1)} %param.14) | copy-start | bytes 3538948
  25.7 13.1 %collective-permute-start = (bf16[32,4,128]{2,1,0:T(4,128)(2,1)S(1)}, bf16[32,4,128]{2,1,0:T(4,128)(2,1)S(1)}, u32[]{:S(2)}, u32[]{:S(2)}) collective-permute-start(bf16[32,4,128]{2,1,0:T(4,128)(2,1)S(1)} %slice.4.freq_ref), channel_id=1, source_target_pairs={{0,64},{64,0},{1,65},{65,1},{2,66},{66,2},{3,67},{67,3},{4,68},{68... | collective-permute-start | bytes 98312 | tf_op jit(solution)/shard_map/ppermute | solution.py:370

commit v4 on v3

--- a/solution.py
+++ b/solution.py
@@ -10,8 +10,11 @@
 SIZES = (4, 2, 2, 2, 2, 2, 4)
 NEAR = ("z2", "z1", "c", "x")
 ALL = ("z4", "z2", "z1", "c", "zh", "x")
+FLIP_NEAR = 2
+FLIP_ALL = 6
 K = 576
 WIDE = 1280
+PACK_VMEM = 60 * 2**20
 COLS = 128
 PIX = 1024
 F32 = jnp.float32
@@ -20,21 +23,18 @@
 VMEM = pl.BlockSpec(memory_space=pltpu.VMEM)
 
 COS = (
-    0.999999989059023,
-    -19.739204499453944,
-    64.9391174598965,
-    -85.45013953089278,
-    60.16763095097771,
-    -25.96759924841038,
-    6.5286581610231424,
+    1.4142134962552286,
+    -6.978850948563802,
+    5.739460376906949,
+    -1.8835579059851506,
+    0.31068802752335445,
 )
 SIN = (
-    6.283184916495431,
-    -41.34158923268858,
-    81.59994332978287,
-    -76.61447253124996,
-    41.34288235456833,
-    -12.471243535026977,
+    4.442882919124345,
+    -7.308245686509067,
+    3.6063542184329913,
+    -0.8461116503747359,
+    0.10982451642751799,
 )
 
 OWN, LOW1, HIGH1, LOW2, HIGH2, ACROSS = range(6)
@@ -157,7 +157,12 @@
     )(nodes, cen, jnp.asarray(CENTRE), jnp.asarray(MASK), jnp.asarray(PICK.reshape(96, 256), BF16))
 
 
-def pack_kernel(coeffs_ref, freqs_ref, out_ref):
+def pack_kernel(coeffs_hbm, freqs_hbm, out_ref, coeffs_ref, freqs_ref, sems):
+    freqs_copy = pltpu.make_async_copy(freqs_hbm, freqs_ref, sems.at[0])
+    coeffs_copy = pltpu.make_async_copy(coeffs_hbm, coeffs_ref, sems.at[1])
+    freqs_copy.start()
+    coeffs_copy.start()
+
     def spread(rows):
         i = lax.broadcasted_iota(jnp.int32, (rows, rows), 0)
         j = lax.broadcasted_iota(jnp.int32, (rows, rows), 1)
@@ -169,23 +174,31 @@
         return z.reshape(32, 4, z.shape[1]).astype(BF16)
 
     whole, tail = spread(256), spread(128)
+    freqs_copy.wait()
+    i = lax.broadcasted_iota(jnp.int32, (10, 128), 0)
+    j = lax.broadcasted_iota(jnp.int32, (10, 128), 1)
+    freqs = freqs_ref[...].astype(F32).reshape(10, COLS).astype(BF16)
+    out_ref[:, :, 1152:] = turned(freqs, jnp.where(i == j, 1.0, 0.0).astype(BF16))
+    coeffs_copy.wait()
     for m in range(4):
         z = turned(coeffs_ref[m * 256 : m * 256 + 256, :], whole)
         out_ref[:, :, m * 128 : m * 128 + 128] = z[:, :, :128]
         out_ref[:, :, 512 + m * 128 : 512 + m * 128 + 128] = z[:, :, 128:]
     out_ref[:, :, 1024:1152] = turned(coeffs_ref[1024:1152, :], tail)
-    i = lax.broadcasted_iota(jnp.int32, (10, 128), 0)
-    j = lax.broadcasted_iota(jnp.int32, (10, 128), 1)
-    out_ref[:, :, 1152:] = turned(freqs_ref[...].astype(F32).reshape(10, COLS).astype(BF16), jnp.where(i == j, 1.0, 0.0).astype(BF16))
 
 
 def pack(coeffs, freqs):
     return pl.pallas_call(
         pack_kernel,
         out_shape=jax.ShapeDtypeStruct((32, 4, WIDE), BF16),
-        in_specs=[VMEM] * 2,
+        in_specs=[pl.BlockSpec(memory_space=pl.ANY)] * 2,
         out_specs=VMEM,
-        compiler_params=pltpu.CompilerParams(vmem_limit_bytes=4 * 2**20),
+        scratch_shapes=[
+            pltpu.VMEM((2 * K, COLS), BF16),
+            pltpu.VMEM((5, 2, COLS), BF16),
+            pltpu.SemaphoreType.DMA((2,)),
+        ],
+        compiler_params=pltpu.CompilerParams(vmem_limit_bytes=PACK_VMEM),
         cost_estimate=pl.CostEstimate(flops=10**7, bytes_accessed=2**20, transcendentals=0),
         name="pack",
     )(coeffs, freqs)
@@ -201,7 +214,8 @@
 def cos_sin(turns):
     r = turns - jnp.floor(turns + 0.5)
     u = r * r
-    return horner(COS, u), r * horner(SIN, u)
+    sine = r * horner(SIN, u)
+    return 1.0 - sine * sine, sine * horner(COS, u)
 
 
 def dot(a, b):
@@ -314,8 +328,10 @@
     phases(placed, table_ref, (HERE, HERE + 1), t_ref)
     v = contribution(s_ref, t_ref, 0, interp_ref[half], w_ref, last_ref)
     for where, value in ((half, v_ref[...]), (1 - half, v)):
-        part = jnp.dot(value, eval_ref[...], preferred_element_type=F32)
-        out_ref[where] = part.astype(BF16)
+        part = jnp.dot(value, eval_ref[...], preferred_element_type=F32).astype(BF16)
+        for p in range(8):
+            member = p ^ FLIP_ALL
+            out_ref[where, :, p * 128 : p * 128 + 128] = part[:, member * 128 : member * 128 + 128]
 
 
 def own_levels(field, freq, table, interp):
@@ -360,19 +376,22 @@
     )(freq, freq_across, v, state, table, interp, evaluate)
 
 
-def exchange(block, axes):
-    return lax.all_to_all(block, axes, split_axis=0, concat_axis=0, tiled=True)
+def exchange(block, axes, flip):
+    groups = [[i ^ flip for i in range(block.shape[0])]]
+    return lax.all_to_all(
+        block, axes, split_axis=0, concat_axis=0, tiled=True, axis_index_groups=groups
+    )
 
 
 def body(coeffs, freqs, nodes, centres, interp, evaluate):
-    field = exchange(pack(coeffs.reshape(2 * K, COLS), freqs[0]), NEAR)
+    field = exchange(pack(coeffs.reshape(2 * K, COLS), freqs[0]), NEAR, FLIP_NEAR)
     freq = field[:, :, WIDE - 128 :]
     freq_across = lax.ppermute(freq, "z4", [(0, 1), (1, 0)])
     table = prepare(nodes.reshape(24, K), centres.reshape(24, 64))
     v, state = own_levels(field, freq, table, interp)
     part = across_level(freq, freq_across, v, state, table, interp, evaluate.T)
     part = part.reshape(16, 4, 8, 128).transpose(0, 2, 1, 3).reshape(128, 4, 128)
-    part = exchange(part, ALL)
+    part = exchange(part, ALL, FLIP_ALL)
     total = jnp.sum(part.reshape(2, 8, 2, 4, 4, 128).astype(F32), axis=(0, 2))
     return total.reshape(COLS, 128).T
 

time: 70.1 us -> 62.7 us (0.89)
  blocking collectives: 28.1 us -> 23.1 us
  waiting for transfers between devices: 8.09 us -> 5.61 us
  local copies, waits for them, and re-layouts: 6.36 us -> 4.71 us
  starting transfers between devices: 18.9 us -> 19.8 us
  Pallas kernels: 8 us -> 8.82 us
    all_to_all x1, blocking collectives: 28.1 us -> 23.1 us  [exchange(): lax.all_to_all(block, axes, split_axis=0, concat_axis=0, tiled=True, axis...]
    all_to_all x1, waiting for transfers between devices: 8.09 us -> 5.61 us  [exchange(): lax.all_to_all(block, axes, split_axis=0, concat_axis=0, tiled=True, axis...]
    unnamed x17 -> x13, local copies, waits for them, and re-layouts: 4.61 us -> 2.97 us
    pallas_call x1, Pallas kernels: 1.02 us -> 2.12 us  [pack(): pl.pallas_call(pack_kernel, out_shape=jax.ShapeDtypeStruct((32, 4, WIDE),...]
    all_to_all x1, starting transfers between devices: 10.4 us -> 11.5 us  [exchange(): lax.all_to_all(block, axes, split_axis=0, concat_axis=0, tiled=True, axis...]
where the time goes in v4:
time: 62.7 us; the launch traced here: 62.2 us
  blocking collectives  23.1 us (37%)
  starting transfers between devices  19.8 us (32%)
  Pallas kernels  8.82 us (14%)
  waiting for transfers between devices  5.61 us (9%)
  local copies, waits for them, and re-layouts  4.71 us (8%)
    all_to_all x1, blocking collectives, exchange(): lax.all_to_all(block, axes, split_axis=0, concat_axis=0, tiled=True, axis...  23.1 us
    all_to_all x1, starting transfers between devices, exchange(): lax.all_to_all(block, axes, split_axis=0, concat_axis=0, tiled=True, axis...  11.5 us
    ppermute x1, starting transfers between devices, body(): freq_across = lax.ppermute(freq, 'z4', [(0, 1), (1, 0)])  8.32 us
    all_to_all x1, waiting for transfers between devices, exchange(): lax.all_to_all(block, axes, split_axis=0, concat_axis=0, tiled=True, axis...  5.61 us
    pallas_call x1, Pallas kernels, own_levels(): pl.pallas_call(own_kernel, out_shape=[jax.ShapeDtypeStruct((32, K), BF16)...  4.42 us
    unnamed x13, local copies, waits for them, and re-layouts  2.97 us
    pallas_call x1, Pallas kernels, pack(): pl.pallas_call(pack_kernel, out_shape=jax.ShapeDtypeStruct((32, 4, WIDE),...  2.12 us
    pallas_call x1, Pallas kernels, across_level(): pl.pallas_call(across_kernel, out_shape=jax.ShapeDtypeStruct((2, 32, PIX)...  1.67 us
  transfers between devices with their start and end apart: 2, of which 1 were waited for; matrix products, arithmetic and copies ran while one was open for 1% of the time, Pallas kernels for 8%

profile of v4, /device:TPU:1, one launch (start us, length us, event | category | flops | bytes accessed | tf_op | source)
XLA Modules:
  0.0 62.2 jit_solution(8108971521821358703)
XLA Ops:
  0.0 0.0 copy-start
  0.0 2.1 %pack.1 = bf16[32,4,1280]{2,1,0:T(4,128)(2,1)} custom-call(bf16[1152,128]{1,0:T(8,128)(2,1)} %bitcast.24, bf16[5,2,128]{2,1,0:T(2,128)(2,1)} %bitcast.26), custom_call_target="tpu_custom_call" | custom-call | flops 10000000 | bytes 1048576 | tf_op jit(solution)/shard_map/pack/pallas_call | solution.py:191
  2.1 11.5 %all-to-all-start = ((bf16[32,4,1280]{2,1,0:T(4,128)(2,1)}), bf16[32,4,1280]{2,1,0:T(4,128)(2,1)S(1)}, u32[]{:S(2)}, u32[]{:S(2)}) async-start(bf16[32,4,1280]{2,1,0:T(4,128)(2,1)} %pack.1), calls=%async_computation | async-start | bytes 655360 | tf_op jit(solution)/shard_map/all_to_all | solution.py:381
  13.6 0.9 %reshape.22.nodes_ref = f32[24,576]{1,0:T(8,128)S(1)} reshape(f32[4,3,2,576]{3,2,1,0:T(2,128)} %param.11) | data formatting | bytes 110592 | tf_op jit(solution)/shard_map/reshape | solution.py:390
  14.5 0.0 copy-start.2
  14.5 0.8 %copy-done.2 = bf16[96,256]{1,0:T(8,128)(2,1)S(1)} copy-done((bf16[96,256]{1,0:T(8,128)(2,1)S(1)}, bf16[96,256]{1,0:T(8,128)(2,1)}, u32[]{:S(2)}) %copy-start.2) | copy-done | bytes 49176
  15.3 0.0 copy-start.3
  15.3 0.7 %copy-done.3 = f32[2,24,128]{2,1,0:T(8,128)S(1)} copy-done((f32[2,24,128]{2,1,0:T(8,128)S(1)}, f32[2,24,128]{2,1,0:T(8,128)}, u32[]{:S(2)}) %copy-start.3) | copy-done | bytes 24600
  16.0 0.0 copy-start.4
  16.1 0.7 %copy-done.4 = f32[4,3,2,64]{3,2,1,0:T(2,128)S(1)} copy-done((f32[4,3,2,64]{3,2,1,0:T(2,128)S(1)}, f32[4,3,2,64]{3,2,1,0:T(2,128)}, u32[]{:S(2)}) %copy-start.4) | copy-done | bytes 6168
  16.8 0.0 copy-start.5
  16.8 0.7 %copy-done.5 = f32[8,128]{1,0:T(8,128)S(1)} copy-done((f32[8,128]{1,0:T(8,128)S(1)}, f32[8,128]{1,0:T(8,128)}, u32[]{:S(2)}) %copy-start.5) | copy-done | bytes 4120
  17.4 0.6 prepare.1.table_ref
  18.1 5.6 %all-to-all-done.field_ref = bf16[32,4,1280]{2,1,0:T(4,128)(2,1)S(1)} async-done(((bf16[32,4,1280]{2,1,0:T(4,128)(2,1)}), bf16[32,4,1280]{2,1,0:T(4,128)(2,1)S(1)}, u32[]{:S(2)}, u32[]{:S(2)}) %all-to-all-start) | async-done | bytes 327712 | tf_op jit(solution)/shard_map/all_to_all | solution.py:381
  23.7 0.0 copy-start.1
  23.7 8.3 %collective-permute-start = (bf16[32,4,128]{2,1,0:T(4,128)(2,1)S(1)}, bf16[32,4,128]{2,1,0:T(4,128)(2,1)S(1)}, u32[]{:S(2)}, u32[]{:S(2)}) collective-permute-start(bf16[32,4,128]{2,1,0:T(4,128)(2,1)S(1)} %slice.4.freq_ref), channel_id=1, source_target_pairs={{0,64},{64,0},{1,65},{65,1},{2,66},{66,2},{3,67},{67,3},{4,68},{68... | collective-permute-start | bytes 98312 | tf_op jit(solution)/shard_map/ppermute | solution.py:389
  32.0 0.0 copy-done
  32.0 4.4 %own_levels.1 = (bf16[32,576]{1,0:T(8,128)(2,1)S(1)}, f32[256,576]{1,0:T(8,128)S(1)}) custom-call(bf16[32,4,1280]{2,1,0:T(4,128)(2,1)S(1)} %all-to-all-done.field_ref, bf16[32,4,128]{2,1,0:T(4,128)(2,1)S(1)} %slice.4.freq_ref, bf16[12,96,576]{2,1,0:T(8,128)(2,1)S(1)} %prepare.1.table_ref, bf16[2,576,576]{2,1,0:T(8,128)(2,1)S(1)} %copy-done), custom_call_target="tpu_custom_call" | custom-call | flops 1358954496 | bytes 10485760 | tf_op jit(solution)/shard_map/own_levels/pallas_call | solution.py:338
  36.5 0.0 collective-permute-done.freq_across_ref
  36.5 0.0 copy-done.1
  36.5 1.7 %across_level.1 = bf16[2,32,1024]{2,1,0:T(8,128)(2,1)S(1)} custom-call(bf16[32,4,128]{2,1,0:T(4,128)(2,1)S(1)} %slice.4.freq_ref, bf16[32,4,128]{2,1,0:T(4,128)(2,1)S(1)} %collective-permute-done.freq_across_ref, bf16[32,576]{1,0:T(8,128)(2,1)S(1)} %get-tuple-element.7.v_ref, f32[256,576]{1,0:T(8,128)S(1)} %get-tuple-element.8.s_ref, ...), custom_call_target="tpu_custom_call" | custom-call | flops 339738624 | bytes 5242880 | tf_op jit(solution)/shard_map/across_level/pallas_call | solution.py:361
  38.2 0.1 copy.13
  38.3 23.1 %all_to_all.10 = bf16[128,4,128]{2,1,0:T(4,128)(2,1)S(1)} all-to-all(bf16[128,4,128]{2,1,0:T(4,128)(2,1)S(1)} %copy.13), channel_id=1, replica_groups={{6,7,4,5,2,3,0,1,14,15,12,13,10,11,8,9,22,23,20,21,18,19,16,17,30,31,28..., dimensions={0} | all-to-all | bytes 262144 | tf_op jit(solution)/shard_map/all_to_all | solution.py:381
  61.4 0.1 convert_reduce_fusion
  61.5 0.7 %copy.16 = f32[128,128]{1,0:T(8,128)} copy(f32[128,128]{0,1:T(8,128)S(1)} %bitcast.25) | data formatting | bytes 131072 | tf_op jit(solution)/shard_map/transpose | solution.py:396
  (3 shorter events, 0.1 us)
Async XLA Ops:
  0.0 32.0 %copy-start = (bf16[2,576,576]{2,1,0:T(8,128)(2,1)S(1)}, bf16[2,576,576]{2,1,0:T(8,128)(2,1)}, u32[]{:S(2)}) copy-start(bf16[2,576,576]{2,1,0:T(8,128)(2,1)} %interp_ref.3) | copy-start | bytes 3981316
  2.1 21.5 %all-to-all-start = ((bf16[32,4,1280]{2,1,0:T(4,128)(2,1)}), bf16[32,4,1280]{2,1,0:T(4,128)(2,1)S(1)}, u32[]{:S(2)}, u32[]{:S(2)}) async-start(bf16[32,4,1280]{2,1,0:T(4,128)(2,1)} %pack.1), calls=%async_computation | async-start | bytes 655360 | tf_op jit(solution)/shard_map/all_to_all | solution.py:381
  14.5 0.8 %copy-start.2 = (bf16[96,256]{1,0:T(8,128)(2,1)S(1)}, bf16[96,256]{1,0:T(8,128)(2,1)}, u32[]{:S(2)}) copy-start(bf16[96,256]{1,0:T(8,128)(2,1)} %constant.10.clone.pick_ref) | copy-start | bytes 147460
  15.3 0.7 %copy-start.3 = (f32[2,24,128]{2,1,0:T(8,128)S(1)}, f32[2,24,128]{2,1,0:T(8,128)}, u32[]{:S(2)}) copy-start(f32[2,24,128]{2,1,0:T(8,128)} %constant.8.clone.centre_ref) | copy-start | bytes 73732
  16.0 0.7 %copy-start.4 = (f32[4,3,2,64]{3,2,1,0:T(2,128)S(1)}, f32[4,3,2,64]{3,2,1,0:T(2,128)}, u32[]{:S(2)}) copy-start(f32[4,3,2,64]{3,2,1,0:T(2,128)} %param.12) | copy-start | bytes 18436
  16.8 0.7 %copy-start.5 = (f32[8,128]{1,0:T(8,128)S(1)}, f32[8,128]{1,0:T(8,128)}, u32[]{:S(2)}) copy-start(f32[8,128]{1,0:T(8,128)} %constant.9.clone.mask_ref) | copy-start | bytes 12292
  23.7 12.8 %copy-start.1 = (bf16[1024,576]{0,1:T(8,128)(2,1)S(1)}, bf16[1024,576]{0,1:T(8,128)(2,1)}, u32[]{:S(2)}) copy-start(bf16[1024,576]{0,1:T(8,128)(2,1)} %param.14) | copy-start | bytes 3538948
  23.7 12.8 %collective-permute-start = (bf16[32,4,128]{2,1,0:T(4,128)(2,1)S(1)}, bf16[32,4,128]{2,1,0:T(4,128)(2,1)S(1)}, u32[]{:S(2)}, u32[]{:S(2)}) collective-permute-start(bf16[32,4,128]{2,1,0:T(4,128)(2,1)S(1)} %slice.4.freq_ref), channel_id=1, source_target_pairs={{0,64},{64,0},{1,65},{65,1},{2,66},{66,2},{3,67},{67,3},{4,68},{68... | collective-permute-start | bytes 98312 | tf_op jit(solution)/shard_map/ppermute | solution.py:389

commit v5 on v4

--- a/solution.py
+++ b/solution.py
@@ -10,8 +10,11 @@
 SIZES = (4, 2, 2, 2, 2, 2, 4)
 NEAR = ("z2", "z1", "c", "x")
 ALL = ("z4", "z2", "z1", "c", "zh", "x")
-FLIP_NEAR = 2
+FLIP_NEAR = 10
 FLIP_ALL = 6
+FLIP_Q = FLIP_NEAR >> 2
+FLIP_BACK = FLIP_ALL >> 3 & 7
+FLIP_CHUNK = FLIP_NEAR ^ (FLIP_BACK << 2 | FLIP_ALL & 3)
 K = 576
 WIDE = 1280
 PACK_VMEM = 60 * 2**20
@@ -95,7 +98,14 @@
 
 
 def moved(q, rows):
-    return {OWN: q, LOW1: q & ~2, HIGH1: q | 2, LOW2: q & ~4, HIGH2: q | 4}[rows]
+    box = q ^ FLIP_Q
+    box = {OWN: box, LOW1: box & ~2, HIGH1: box | 2, LOW2: box & ~4, HIGH2: box | 4}[rows]
+    return box ^ FLIP_Q
+
+
+def child(q, level, kind):
+    box = q ^ FLIP_Q
+    return ((box & ~(1 << level)) | (kind << level)) ^ FLIP_Q
 
 
 def prepare_kernel(nodes_ref, cen_ref, centre_ref, mask_ref, pick_ref, out_ref, wide_ref):
@@ -129,7 +139,7 @@
         precision=HIGHEST,
         preferred_element_type=F32,
     )
-    q = lax.broadcasted_iota(jnp.int32, (32, 64), 0) & 7
+    q = lax.broadcasted_iota(jnp.int32, (32, 64), 0) & 7 ^ FLIP_Q
     lane = lax.broadcasted_iota(jnp.int32, (32, 64), 1)
     own = base + half * 8
     across = base + 8 - half * 8
@@ -171,7 +181,10 @@
 
     def turned(x, y):
         z = lax.dot_general(x, y, (((0,), (0,)), ((), ())), preferred_element_type=F32)
-        return z.reshape(32, 4, z.shape[1]).astype(BF16)
+        z = z.reshape(32, 4, z.shape[1])
+        if FLIP_CHUNK:
+            z = jnp.concatenate([z[i ^ FLIP_CHUNK : (i ^ FLIP_CHUNK) + 1] for i in range(32)], axis=0)
+        return z.astype(BF16)
 
     whole, tail = spread(256), spread(128)
     freqs_copy.wait()
@@ -266,7 +279,8 @@
         w_ref[here, :] = v.astype(BF16)
     a = lax.broadcasted_iota(jnp.int32, (32, COLS), 0)
     b = lax.broadcasted_iota(jnp.int32, (32, COLS), 1)
-    angles = jnp.where((a // 4 == b // 16) & (a % 4 == b % 4), 1.0, 0.0).astype(BF16)
+    box = b // 16 ^ FLIP_Q ^ FLIP_BACK
+    angles = jnp.where((a // 4 == box) & (a % 4 == b % 4), 1.0, 0.0).astype(BF16)
     return jnp.dot(angles, w_ref[:COLS, :], preferred_element_type=F32).astype(BF16)
 
 
@@ -295,7 +309,7 @@
         for q in range(8):
             here = block(q)
             for kind, w_ref in enumerate((low_ref, high_ref)):
-                src = (q & ~(1 << level)) | (kind << level)
+                src = child(q, level, kind)
                 if level == 0:
                     re, im = fields(field_ref, src)
                 else:
@@ -323,15 +337,17 @@
     t_ref,
 ):
     half = lax.axis_index("z4")
+    place = half ^ (FLIP_ALL >> 6)
     placed = picked(table_ref, OWN, lanes_16(freq_ref))
     placed = placed + picked(table_ref, ACROSS, lanes_16(freq_across_ref))
     phases(placed, table_ref, (HERE, HERE + 1), t_ref)
     v = contribution(s_ref, t_ref, 0, interp_ref[half], w_ref, last_ref)
-    for where, value in ((half, v_ref[...]), (1 - half, v)):
-        part = jnp.dot(value, eval_ref[...], preferred_element_type=F32).astype(BF16)
+    for where, value in ((place, v_ref[...]), (1 - place, v)):
+        part = jnp.dot(value, eval_ref[...], preferred_element_type=F32)
+        part = part.reshape(8, 4, PIX).astype(BF16)
         for p in range(8):
-            member = p ^ FLIP_ALL
-            out_ref[where, :, p * 128 : p * 128 + 128] = part[:, member * 128 : member * 128 + 128]
+            member = p ^ FLIP_ALL & 7
+            out_ref[where, :, p] = part[:, :, member * 128 : member * 128 + 128]
 
 
 def own_levels(field, freq, table, interp):
@@ -360,7 +376,7 @@
 def across_level(freq, freq_across, v, state, table, interp, evaluate):
     return pl.pallas_call(
         across_kernel,
-        out_shape=jax.ShapeDtypeStruct((2, 32, PIX), BF16),
+        out_shape=jax.ShapeDtypeStruct((2, 8, 8, 4, 128), BF16),
         in_specs=[VMEM] * 7,
         out_specs=VMEM,
         scratch_shapes=[
@@ -390,7 +406,7 @@
     table = prepare(nodes.reshape(24, K), centres.reshape(24, 64))
     v, state = own_levels(field, freq, table, interp)
     part = across_level(freq, freq_across, v, state, table, interp, evaluate.T)
-    part = part.reshape(16, 4, 8, 128).transpose(0, 2, 1, 3).reshape(128, 4, 128)
+    part = part.reshape(128, 4, 128)
     part = exchange(part, ALL, FLIP_ALL)
     total = jnp.sum(part.reshape(2, 8, 2, 4, 4, 128).astype(F32), axis=(0, 2))
     return total.reshape(COLS, 128).T

time: 62.7 us -> 61.5 us (0.981)
  waiting for transfers between devices: 5.61 us -> 4.76 us
    all_to_all x1, starting transfers between devices: 11.5 us -> 12.4 us  [exchange(): lax.all_to_all(block, axes, split_axis=0, concat_axis=0, tiled=True, axis...]
    ppermute x1, starting transfers between devices: 8.32 us -> 7.42 us  [body(): freq_across = lax.ppermute(freq, 'z4', [(0, 1), (1, 0)])]
    all_to_all x1, waiting for transfers between devices: 5.61 us -> 4.76 us  [exchange(): lax.all_to_all(block, axes, split_axis=0, concat_axis=0, tiled=True, axis...]
    unnamed x13 -> x12, local copies, waits for them, and re-layouts: 2.97 us -> 2.93 us
where the time goes in v5:
time: 61.5 us; the launch traced here: 61 us
  blocking collectives  22.9 us (37%)
  starting transfers between devices  19.8 us (32%)
  Pallas kernels  8.84 us (14%)
  waiting for transfers between devices  4.76 us (8%)
  local copies, waits for them, and re-layouts  4.55 us (7%)
    all_to_all x1, blocking collectives, exchange(): lax.all_to_all(block, axes, split_axis=0, concat_axis=0, tiled=True, axis...  22.9 us
    all_to_all x1, starting transfers between devices, exchange(): lax.all_to_all(block, axes, split_axis=0, concat_axis=0, tiled=True, axis...  12.4 us
    ppermute x1, starting transfers between devices, body(): freq_across = lax.ppermute(freq, 'z4', [(0, 1), (1, 0)])  7.42 us
    all_to_all x1, waiting for transfers between devices, exchange(): lax.all_to_all(block, axes, split_axis=0, concat_axis=0, tiled=True, axis...  4.76 us
    pallas_call x1, Pallas kernels, own_levels(): pl.pallas_call(own_kernel, out_shape=[jax.ShapeDtypeStruct((32, K), BF16)...  4.42 us
    unnamed x12, local copies, waits for them, and re-layouts  2.93 us
    pallas_call x1, Pallas kernels, pack(): pl.pallas_call(pack_kernel, out_shape=jax.ShapeDtypeStruct((32, 4, WIDE),...  2.12 us
    pallas_call x1, Pallas kernels, across_level(): pl.pallas_call(across_kernel, out_shape=jax.ShapeDtypeStruct((2, 8, 8, 4,...  1.68 us
  transfers between devices with their start and end apart: 2, of which 1 were waited for; matrix products, arithmetic and copies ran while one was open for 1% of the time, Pallas kernels for 8%

profile of v5, /device:TPU:1, one launch (start us, length us, event | category | flops | bytes accessed | tf_op | source)
XLA Modules:
  0.0 61.0 jit_solution(7684407978754121979)
XLA Ops:
  0.0 0.0 copy-start
  0.0 2.1 %pack.1 = bf16[32,4,1280]{2,1,0:T(4,128)(2,1)} custom-call(bf16[1152,128]{1,0:T(8,128)(2,1)} %bitcast.14, bf16[5,2,128]{2,1,0:T(2,128)(2,1)} %bitcast.16), custom_call_target="tpu_custom_call" | custom-call | flops 10000000 | bytes 1048576 | tf_op jit(solution)/shard_map/pack/pallas_call | solution.py:204
  2.1 12.4 %all-to-all-start = ((bf16[32,4,1280]{2,1,0:T(4,128)(2,1)}), bf16[32,4,1280]{2,1,0:T(4,128)(2,1)S(1)}, u32[]{:S(2)}, u32[]{:S(2)}) async-start(bf16[32,4,1280]{2,1,0:T(4,128)(2,1)} %pack.1), calls=%async_computation | async-start | bytes 655360 | tf_op jit(solution)/shard_map/all_to_all | solution.py:397
  14.5 0.9 %reshape.19.nodes_ref = f32[24,576]{1,0:T(8,128)S(1)} reshape(f32[4,3,2,576]{3,2,1,0:T(2,128)} %param.11) | data formatting | bytes 110592 | tf_op jit(solution)/shard_map/reshape | solution.py:406
  15.4 0.0 copy-start.2
  15.4 0.8 %copy-done.2 = bf16[96,256]{1,0:T(8,128)(2,1)S(1)} copy-done((bf16[96,256]{1,0:T(8,128)(2,1)S(1)}, bf16[96,256]{1,0:T(8,128)(2,1)}, u32[]{:S(2)}) %copy-start.2) | copy-done | bytes 49176
  16.2 0.0 copy-start.3
  16.2 0.7 %copy-done.3 = f32[2,24,128]{2,1,0:T(8,128)S(1)} copy-done((f32[2,24,128]{2,1,0:T(8,128)S(1)}, f32[2,24,128]{2,1,0:T(8,128)}, u32[]{:S(2)}) %copy-start.3) | copy-done | bytes 24600
  17.0 0.0 copy-start.4
  17.0 0.7 %copy-done.4 = f32[4,3,2,64]{3,2,1,0:T(2,128)S(1)} copy-done((f32[4,3,2,64]{3,2,1,0:T(2,128)S(1)}, f32[4,3,2,64]{3,2,1,0:T(2,128)}, u32[]{:S(2)}) %copy-start.4) | copy-done | bytes 6168
  17.7 0.0 copy-start.5
  17.7 0.7 %copy-done.5 = f32[8,128]{1,0:T(8,128)S(1)} copy-done((f32[8,128]{1,0:T(8,128)S(1)}, f32[8,128]{1,0:T(8,128)}, u32[]{:S(2)}) %copy-start.5) | copy-done | bytes 4120
  18.3 0.6 %prepare.1.table_ref = bf16[12,96,576]{2,1,0:T(8,128)(2,1)S(1)} custom-call(f32[24,576]{1,0:T(8,128)S(1)} %reshape.19.nodes_ref, f32[24,64]{1,0:T(8,128)S(1)} %bitcast.12, f32[2,24,128]{2,1,0:T(8,128)S(1)} %copy-done.3, f32[8,128]{1,0:T(8,128)S(1)} %copy-done.5, bf16[96,256]{1,0:T(8,128)(2,1)S(1)} %copy-done.2), custom_call_target="tpu_custom_call" | custom-call | flops 10000000 | bytes 5242880 | tf_op jit(solution)/shard_map/prepare/pallas_call | solution.py:158
  19.0 4.8 %all-to-all-done.field_ref = bf16[32,4,1280]{2,1,0:T(4,128)(2,1)S(1)} async-done(((bf16[32,4,1280]{2,1,0:T(4,128)(2,1)}), bf16[32,4,1280]{2,1,0:T(4,128)(2,1)S(1)}, u32[]{:S(2)}, u32[]{:S(2)}) %all-to-all-start) | async-done | bytes 327712 | tf_op jit(solution)/shard_map/all_to_all | solution.py:397
  23.7 0.0 copy-start.1
  23.8 7.4 %collective-permute-start = (bf16[32,4,128]{2,1,0:T(4,128)(2,1)S(1)}, bf16[32,4,128]{2,1,0:T(4,128)(2,1)S(1)}, u32[]{:S(2)}, u32[]{:S(2)}) collective-permute-start(bf16[32,4,128]{2,1,0:T(4,128)(2,1)S(1)} %slice.4.freq_ref), channel_id=1, source_target_pairs={{0,64},{64,0},{1,65},{65,1},{2,66},{66,2},{3,67},{67,3},{4,68},{68... | collective-permute-start | bytes 98312 | tf_op jit(solution)/shard_map/ppermute | solution.py:405
  31.2 0.0 copy-done
  31.2 4.4 %own_levels.1 = (bf16[32,576]{1,0:T(8,128)(2,1)S(1)}, f32[256,576]{1,0:T(8,128)S(1)}) custom-call(bf16[32,4,1280]{2,1,0:T(4,128)(2,1)S(1)} %all-to-all-done.field_ref, bf16[32,4,128]{2,1,0:T(4,128)(2,1)S(1)} %slice.4.freq_ref, bf16[12,96,576]{2,1,0:T(8,128)(2,1)S(1)} %prepare.1.table_ref, bf16[2,576,576]{2,1,0:T(8,128)(2,1)S(1)} %copy-done), custom_call_target="tpu_custom_call" | custom-call | flops 1358954496 | bytes 10485760 | tf_op jit(solution)/shard_map/own_levels/pallas_call | solution.py:354
  35.6 0.0 collective-permute-done.freq_across_ref
  35.6 0.0 copy-done.1
  35.6 1.7 %across_level.1 = bf16[2,8,8,4,128]{4,3,2,1,0:T(4,128)(2,1)S(1)} custom-call(bf16[32,4,128]{2,1,0:T(4,128)(2,1)S(1)} %slice.4.freq_ref, bf16[32,4,128]{2,1,0:T(4,128)(2,1)S(1)} %collective-permute-done.freq_across_ref, bf16[32,576]{1,0:T(8,128)(2,1)S(1)} %get-tuple-element.7.v_ref, f32[256,576]{1,0:T(8,128)S(1)} %get-tuple-element.8.s_ref, ...), custom_call_target="tpu_custom_call" | custom-call | flops 339738624 | bytes 5242880 | tf_op jit(solution)/shard_map/across_level/pallas_call | solution.py:377
  37.3 22.9 %all_to_all.10 = bf16[128,4,128]{2,1,0:T(4,128)(2,1)S(1)} all-to-all(bf16[128,4,128]{2,1,0:T(4,128)(2,1)S(1)} %bitcast.11), channel_id=1, replica_groups={{6,7,4,5,2,3,0,1,14,15,12,13,10,11,8,9,22,23,20,21,18,19,16,17,30,31,28..., dimensions={0} | all-to-all | bytes 262144 | tf_op jit(solution)/shard_map/all_to_all | solution.py:397
  60.2 0.1 convert_reduce_fusion
  60.3 0.7 %copy.10 = f32[128,128]{1,0:T(8,128)} copy(f32[128,128]{0,1:T(8,128)S(1)} %bitcast.15) | data formatting | bytes 131072 | tf_op jit(solution)/shard_map/transpose | solution.py:412
  (1 shorter events, 0.0 us)
Async XLA Ops:
  0.0 31.2 %copy-start = (bf16[2,576,576]{2,1,0:T(8,128)(2,1)S(1)}, bf16[2,576,576]{2,1,0:T(8,128)(2,1)}, u32[]{:S(2)}) copy-start(bf16[2,576,576]{2,1,0:T(8,128)(2,1)} %interp_ref.3) | copy-start | bytes 3981316
  2.1 21.6 %all-to-all-start = ((bf16[32,4,1280]{2,1,0:T(4,128)(2,1)}), bf16[32,4,1280]{2,1,0:T(4,128)(2,1)S(1)}, u32[]{:S(2)}, u32[]{:S(2)}) async-start(bf16[32,4,1280]{2,1,0:T(4,128)(2,1)} %pack.1), calls=%async_computation | async-start | bytes 655360 | tf_op jit(solution)/shard_map/all_to_all | solution.py:397
  15.4 0.8 %copy-start.2 = (bf16[96,256]{1,0:T(8,128)(2,1)S(1)}, bf16[96,256]{1,0:T(8,128)(2,1)}, u32[]{:S(2)}) copy-start(bf16[96,256]{1,0:T(8,128)(2,1)} %constant.10.clone.pick_ref) | copy-start | bytes 147460
  16.2 0.7 %copy-start.3 = (f32[2,24,128]{2,1,0:T(8,128)S(1)}, f32[2,24,128]{2,1,0:T(8,128)}, u32[]{:S(2)}) copy-start(f32[2,24,128]{2,1,0:T(8,128)} %constant.8.clone.centre_ref) | copy-start | bytes 73732
  17.0 0.7 %copy-start.4 = (f32[4,3,2,64]{3,2,1,0:T(2,128)S(1)}, f32[4,3,2,64]{3,2,1,0:T(2,128)}, u32[]{:S(2)}) copy-start(f32[4,3,2,64]{3,2,1,0:T(2,128)} %param.12) | copy-start | bytes 18436
  17.7 0.7 %copy-start.5 = (f32[8,128]{1,0:T(8,128)S(1)}, f32[8,128]{1,0:T(8,128)}, u32[]{:S(2)}) copy-start(f32[8,128]{1,0:T(8,128)} %constant.9.clone.mask_ref) | copy-start | bytes 12292
  23.7 11.9 %copy-start.1 = (bf16[1024,576]{0,1:T(8,128)(2,1)S(1)}, bf16[1024,576]{0,1:T(8,128)(2,1)}, u32[]{:S(2)}) copy-start(bf16[1024,576]{0,1:T(8,128)(2,1)} %param.14) | copy-start | bytes 3538948
  23.8 11.9 %collective-permute-start = (bf16[32,4,128]{2,1,0:T(4,128)(2,1)S(1)}, bf16[32,4,128]{2,1,0:T(4,128)(2,1)S(1)}, u32[]{:S(2)}, u32[]{:S(2)}) collective-permute-start(bf16[32,4,128]{2,1,0:T(4,128)(2,1)S(1)} %slice.4.freq_ref), channel_id=1, source_target_pairs={{0,64},{64,0},{1,65},{65,1},{2,66},{66,2},{3,67},{67,3},{4,68},{68... | collective-permute-start | bytes 98312 | tf_op jit(solution)/shard_map/ppermute | solution.py:405

commit v6 on v5

--- a/solution.py
+++ b/solution.py
@@ -15,6 +15,7 @@
 FLIP_Q = FLIP_NEAR >> 2
 FLIP_BACK = FLIP_ALL >> 3 & 7
 FLIP_CHUNK = FLIP_NEAR ^ (FLIP_BACK << 2 | FLIP_ALL & 3)
+SPOTS = 16
 K = 576
 WIDE = 1280
 PACK_VMEM = 60 * 2**20
@@ -84,6 +85,9 @@
         for i, term in enumerate(TERMS):
             if term[2] == lane:
                 pick[rows, at, 128 + i] = 1
+    spots = np.zeros((96, 256), np.float32)
+    for i in range(64):
+        spots[i] = pick[ACROSS, 6 + i % 4]
     centre = np.zeros((2, 24, 128), np.float32)
     mask = np.zeros((8, 128), np.float32)
     for i, (s, sign, lane, level, kind, d) in enumerate(TERMS):
@@ -91,6 +95,7 @@
             k = half if kind is None else kind
             centre[half, (level * 3 + k) * 2 + d, i] = sign
         mask[FREQS[lane][0], i] = 1
+    pick = np.concatenate([pick.reshape(96, 256), spots], axis=1)
     return pick, centre, mask
 
 
@@ -151,7 +156,7 @@
         total = total + mine * mask_ref[v : v + 1, :]
     for piece, part in pieces(total):
         out_ref[10, 32 * piece : 32 * piece + 32, :128] = part
-    out_ref[11, :, :256] = pick_ref[...]
+    out_ref[11, :, :512] = pick_ref[...]
 
 
 def prepare(nodes, cen):
@@ -164,7 +169,7 @@
         compiler_params=pltpu.CompilerParams(vmem_limit_bytes=6 * 2**20),
         cost_estimate=pl.CostEstimate(flops=10**7, bytes_accessed=5 * 2**20, transcendentals=0),
         name="prepare",
-    )(nodes, cen, jnp.asarray(CENTRE), jnp.asarray(MASK), jnp.asarray(PICK.reshape(96, 256), BF16))
+    )(nodes, cen, jnp.asarray(CENTRE), jnp.asarray(MASK), jnp.asarray(PICK, BF16))
 
 
 def pack_kernel(coeffs_hbm, freqs_hbm, out_ref, coeffs_ref, freqs_ref, sems):
@@ -190,8 +195,11 @@
     freqs_copy.wait()
     i = lax.broadcasted_iota(jnp.int32, (10, 128), 0)
     j = lax.broadcasted_iota(jnp.int32, (10, 128), 1)
+    position = lax.axis_index(NEAR) ^ FLIP_NEAR
+    spot = SPOTS + 4 * (position & 15)
+    hot = (i == j) | ((i > 5) & (j == i - 6 + spot))
     freqs = freqs_ref[...].astype(F32).reshape(10, COLS).astype(BF16)
-    out_ref[:, :, 1152:] = turned(freqs, jnp.where(i == j, 1.0, 0.0).astype(BF16))
+    out_ref[:, :, 1152:] = turned(freqs, jnp.where(hot, 1.0, 0.0).astype(BF16))
     coeffs_copy.wait()
     for m in range(4):
         z = turned(coeffs_ref[m * 256 : m * 256 + 256, :], whole)
@@ -239,6 +247,13 @@
     return slice(q * 16, q * 16 + 16)
 
 
+def pieces(rest):
+    for _ in range(3):
+        part = rest.astype(BF16)
+        yield part
+        rest = rest - part.astype(F32)
+
+
 def picked(table_ref, rows, freq):
     pick = table_ref[11, 16 * rows : 16 * rows + 16, :256]
     return jnp.dot(freq, pick, preferred_element_type=F32)
@@ -255,7 +270,10 @@
     centre = jnp.concatenate(
         [jnp.broadcast_to(centre[q : q + 1], (16, 128)) for q in range(8)], axis=0
     )
-    const = jnp.dot(placed[:, 128:] * centre, gather, precision=HIGHEST, preferred_element_type=F32)
+    const = sum(
+        jnp.dot(part, gather.astype(BF16), preferred_element_type=F32)
+        for part in pieces(placed[:, 128:] * centre)
+    )
     for i, s in enumerate(sets):
         t_ref[i] = jnp.dot(lanes, table_ref[s], preferred_element_type=F32) + const[:, s : s + 1]
 
@@ -339,7 +357,13 @@
     half = lax.axis_index("z4")
     place = half ^ (FLIP_ALL >> 6)
     placed = picked(table_ref, OWN, lanes_16(freq_ref))
-    placed = placed + picked(table_ref, ACROSS, lanes_16(freq_across_ref))
+    across = freq_across_ref[...].astype(F32)[:, None]
+    across = jnp.broadcast_to(across, (2, 16, 4, 128)).reshape(COLS, 128)
+    across = across[:, SPOTS : SPOTS + 64]
+    a = lax.broadcasted_iota(jnp.int32, (COLS, 64), 0)
+    b = lax.broadcasted_iota(jnp.int32, (COLS, 64), 1)
+    across = jnp.where(a // 4 % 16 == b // 4, across, 0.0).astype(BF16)
+    placed = placed + jnp.dot(across, table_ref[11, :64, 256:512], preferred_element_type=F32)
     phases(placed, table_ref, (HERE, HERE + 1), t_ref)
     v = contribution(s_ref, t_ref, 0, interp_ref[half], w_ref, last_ref)
     for where, value in ((place, v_ref[...]), (1 - place, v)):
@@ -402,7 +426,8 @@
 def body(coeffs, freqs, nodes, centres, interp, evaluate):
     field = exchange(pack(coeffs.reshape(2 * K, COLS), freqs[0]), NEAR, FLIP_NEAR)
     freq = field[:, :, WIDE - 128 :]
-    freq_across = lax.ppermute(freq, "z4", [(0, 1), (1, 0)])
+    spots = jnp.sum(freq.reshape(2, 16, 4, 128).astype(F32), axis=1).astype(BF16)
+    freq_across = lax.ppermute(spots, "z4", [(0, 1), (1, 0)])
     table = prepare(nodes.reshape(24, K), centres.reshape(24, 64))
     v, state = own_levels(field, freq, table, interp)
     part = across_level(freq, freq_across, v, state, table, interp, evaluate.T)

time: 61.5 us -> 61.3 us (level)
  local copies, waits for them, and re-layouts: 4.55 us -> 3.76 us
  waiting for transfers between devices: 4.76 us -> 5.55 us
    unnamed x12, local copies, waits for them, and re-layouts: 2.93 us -> 2.14 us
    all_to_all x1, waiting for transfers between devices: 4.76 us -> 5.54 us  [exchange(): lax.all_to_all(block, axes, split_axis=0, concat_axis=0, tiled=True, axis...]
where the time goes in v6:
time: 61.3 us; the launch traced here: 60.9 us
  blocking collectives  22.9 us (37%)
  starting transfers between devices  19.7 us (32%)
  Pallas kernels  8.85 us (14%)
  waiting for transfers between devices  5.55 us (9%)
  local copies, waits for them, and re-layouts  3.76 us (6%)
    all_to_all x1, blocking collectives, exchange(): lax.all_to_all(block, axes, split_axis=0, concat_axis=0, tiled=True, axis...  22.9 us
    all_to_all x1, starting transfers between devices, exchange(): lax.all_to_all(block, axes, split_axis=0, concat_axis=0, tiled=True, axis...  12.4 us
    ppermute x1, starting transfers between devices, body(): freq_across = lax.ppermute(spots, 'z4', [(0, 1), (1, 0)])  7.3 us
    all_to_all x1, waiting for transfers between devices, exchange(): lax.all_to_all(block, axes, split_axis=0, concat_axis=0, tiled=True, axis...  5.54 us
    pallas_call x1, Pallas kernels, own_levels(): pl.pallas_call(own_kernel, out_shape=[jax.ShapeDtypeStruct((32, K), BF16)...  4.43 us
    unnamed x12, local copies, waits for them, and re-layouts  2.14 us
    pallas_call x1, Pallas kernels, pack(): pl.pallas_call(pack_kernel, out_shape=jax.ShapeDtypeStruct((32, 4, WIDE),...  2.11 us
    pallas_call x1, Pallas kernels, across_level(): pl.pallas_call(across_kernel, out_shape=jax.ShapeDtypeStruct((2, 8, 8, 4,...  1.69 us
  transfers between devices with their start and end apart: 2, of which 1 were waited for; matrix products, arithmetic and copies ran while one was open for 1% of the time, Pallas kernels for 8%

profile of v6, /device:TPU:1, one launch (start us, length us, event | category | flops | bytes accessed | tf_op | source)
XLA Modules:
  0.0 60.9 jit_solution(352321592096642539)
XLA Ops:
  0.0 0.0 copy-start.2
  0.0 0.0 copy-start
  0.0 2.1 %pack.1 = bf16[32,4,1280]{2,1,0:T(4,128)(2,1)} custom-call(bf16[1152,128]{1,0:T(8,128)(2,1)} %bitcast.16, bf16[5,2,128]{2,1,0:T(2,128)(2,1)} %bitcast.18), custom_call_target="tpu_custom_call" | custom-call | flops 10000000 | bytes 1048576 | tf_op jit(solution)/shard_map/pack/pallas_call | solution.py:212
  2.1 12.4 %all-to-all-start = ((bf16[32,4,1280]{2,1,0:T(4,128)(2,1)}), bf16[32,4,1280]{2,1,0:T(4,128)(2,1)S(1)}, u32[]{:S(2)}, u32[]{:S(2)}) async-start(bf16[32,4,1280]{2,1,0:T(4,128)(2,1)} %pack.1), calls=%async_computation | async-start | bytes 655360 | tf_op jit(solution)/shard_map/all_to_all | solution.py:421
  14.5 0.9 %reshape.23.nodes_ref = f32[24,576]{1,0:T(8,128)S(1)} reshape(f32[4,3,2,576]{3,2,1,0:T(2,128)} %param.11) | data formatting | bytes 110592 | tf_op jit(solution)/shard_map/reshape | solution.py:431
  15.4 0.0 copy-done.2
  15.4 0.0 copy-start.3
  15.4 0.7 %copy-done.3 = f32[2,24,128]{2,1,0:T(8,128)S(1)} copy-done((f32[2,24,128]{2,1,0:T(8,128)S(1)}, f32[2,24,128]{2,1,0:T(8,128)}, u32[]{:S(2)}) %copy-start.3) | copy-done | bytes 24600
  16.2 0.0 copy-start.4
  16.2 0.7 %copy-done.4 = f32[4,3,2,64]{3,2,1,0:T(2,128)S(1)} copy-done((f32[4,3,2,64]{3,2,1,0:T(2,128)S(1)}, f32[4,3,2,64]{3,2,1,0:T(2,128)}, u32[]{:S(2)}) %copy-start.4) | copy-done | bytes 6168
  16.9 0.0 copy-start.5
  16.9 0.7 %copy-done.5 = f32[8,128]{1,0:T(8,128)S(1)} copy-done((f32[8,128]{1,0:T(8,128)S(1)}, f32[8,128]{1,0:T(8,128)}, u32[]{:S(2)}) %copy-start.5) | copy-done | bytes 4120
  17.5 0.6 %prepare.1.table_ref = bf16[12,96,576]{2,1,0:T(8,128)(2,1)S(1)} custom-call(f32[24,576]{1,0:T(8,128)S(1)} %reshape.23.nodes_ref, f32[24,64]{1,0:T(8,128)S(1)} %bitcast.14, f32[2,24,128]{2,1,0:T(8,128)S(1)} %copy-done.3, f32[8,128]{1,0:T(8,128)S(1)} %copy-done.5, bf16[96,512]{1,0:T(8,128)(2,1)S(1)} %copy-done.2), custom_call_target="tpu_custom_call" | custom-call | flops 10000000 | bytes 5242880 | tf_op jit(solution)/shard_map/prepare/pallas_call | solution.py:163
  18.2 5.5 %all-to-all-done.field_ref = bf16[32,4,1280]{2,1,0:T(4,128)(2,1)S(1)} async-done(((bf16[32,4,1280]{2,1,0:T(4,128)(2,1)}), bf16[32,4,1280]{2,1,0:T(4,128)(2,1)S(1)}, u32[]{:S(2)}, u32[]{:S(2)}) %all-to-all-start) | async-done | bytes 327712 | tf_op jit(solution)/shard_map/all_to_all | solution.py:421
  23.7 7.3 %collective-permute-start = (bf16[2,4,128]{2,1,0:T(4,128)(2,1)S(1)}, bf16[2,4,128]{2,1,0:T(4,128)(2,1)S(1)}, u32[]{:S(2)}, u32[]{:S(2)}) collective-permute-start(bf16[2,4,128]{2,1,0:T(4,128)(2,1)S(1)} %bitcast_reduce_fusion), channel_id=1, source_target_pairs={{0,64},{64,0},{1,65},{65,1},{2,66},{66,2},{3,67},{67,3},{4,68},{68... | collective-permute-start | bytes 6152 | tf_op jit(solution)/shard_map/ppermute | solution.py:430
  31.1 0.0 copy-done
  31.1 0.0 copy-start.1
  31.1 4.4 %own_levels.1 = (bf16[32,576]{1,0:T(8,128)(2,1)S(1)}, f32[256,576]{1,0:T(8,128)S(1)}) custom-call(bf16[32,4,1280]{2,1,0:T(4,128)(2,1)S(1)} %all-to-all-done.field_ref, bf16[32,4,128]{2,1,0:T(4,128)(2,1)S(1)} %slice.4.freq_ref, bf16[12,96,576]{2,1,0:T(8,128)(2,1)S(1)} %prepare.1.table_ref, bf16[2,576,576]{2,1,0:T(8,128)(2,1)S(1)} %copy-done), custom_call_target="tpu_custom_call" | custom-call | flops 1358954496 | bytes 10485760 | tf_op jit(solution)/shard_map/own_levels/pallas_call | solution.py:378
  35.5 0.0 collective-permute-done.freq_across_ref
  35.5 0.0 copy-done.1
  35.5 1.7 %across_level.1 = bf16[2,8,8,4,128]{4,3,2,1,0:T(4,128)(2,1)S(1)} custom-call(bf16[32,4,128]{2,1,0:T(4,128)(2,1)S(1)} %slice.4.freq_ref, bf16[2,4,128]{2,1,0:T(4,128)(2,1)S(1)} %collective-permute-done.freq_across_ref, bf16[32,576]{1,0:T(8,128)(2,1)S(1)} %get-tuple-element.7.v_ref, f32[256,576]{1,0:T(8,128)S(1)} %get-tuple-element.8.s_ref, ...), custom_call_target="tpu_custom_call" | custom-call | flops 339738624 | bytes 5242880 | tf_op jit(solution)/shard_map/across_level/pallas_call | solution.py:401
  37.2 22.9 %all_to_all.10 = bf16[128,4,128]{2,1,0:T(4,128)(2,1)S(1)} all-to-all(bf16[128,4,128]{2,1,0:T(4,128)(2,1)S(1)} %bitcast.13), channel_id=1, replica_groups={{6,7,4,5,2,3,0,1,14,15,12,13,10,11,8,9,22,23,20,21,18,19,16,17,30,31,28..., dimensions={0} | all-to-all | bytes 262144 | tf_op jit(solution)/shard_map/all_to_all | solution.py:421
  60.1 0.1 convert_reduce_fusion
  60.1 0.7 %copy.10 = f32[128,128]{1,0:T(8,128)} copy(f32[128,128]{0,1:T(8,128)S(1)} %bitcast.17) | data formatting | bytes 131072 | tf_op jit(solution)/shard_map/transpose | solution.py:437
  (2 shorter events, 0.0 us)
Async XLA Ops:
  0.0 15.4 %copy-start.2 = (bf16[96,512]{1,0:T(8,128)(2,1)S(1)}, bf16[96,512]{1,0:T(8,128)(2,1)}, u32[]{:S(2)}) copy-start(bf16[96,512]{1,0:T(8,128)(2,1)} %constant.12.clone.pick_ref) | copy-start | bytes 294916
  0.0 31.1 %copy-start = (bf16[2,576,576]{2,1,0:T(8,128)(2,1)S(1)}, bf16[2,576,576]{2,1,0:T(8,128)(2,1)}, u32[]{:S(2)}) copy-start(bf16[2,576,576]{2,1,0:T(8,128)(2,1)} %interp_ref.3) | copy-start | bytes 3981316
  2.1 21.6 %all-to-all-start = ((bf16[32,4,1280]{2,1,0:T(4,128)(2,1)}), bf16[32,4,1280]{2,1,0:T(4,128)(2,1)S(1)}, u32[]{:S(2)}, u32[]{:S(2)}) async-start(bf16[32,4,1280]{2,1,0:T(4,128)(2,1)} %pack.1), calls=%async_computation | async-start | bytes 655360 | tf_op jit(solution)/shard_map/all_to_all | solution.py:421
  15.4 0.7 %copy-start.3 = (f32[2,24,128]{2,1,0:T(8,128)S(1)}, f32[2,24,128]{2,1,0:T(8,128)}, u32[]{:S(2)}) copy-start(f32[2,24,128]{2,1,0:T(8,128)} %constant.10.clone.centre_ref) | copy-start | bytes 73732
  16.2 0.7 %copy-start.4 = (f32[4,3,2,64]{3,2,1,0:T(2,128)S(1)}, f32[4,3,2,64]{3,2,1,0:T(2,128)}, u32[]{:S(2)}) copy-start(f32[4,3,2,64]{3,2,1,0:T(2,128)} %param.12) | copy-start | bytes 18436
  16.9 0.7 %copy-start.5 = (f32[8,128]{1,0:T(8,128)S(1)}, f32[8,128]{1,0:T(8,128)}, u32[]{:S(2)}) copy-start(f32[8,128]{1,0:T(8,128)} %constant.11.clone.mask_ref) | copy-start | bytes 12292
  23.7 11.8 %collective-permute-start = (bf16[2,4,128]{2,1,0:T(4,128)(2,1)S(1)}, bf16[2,4,128]{2,1,0:T(4,128)(2,1)S(1)}, u32[]{:S(2)}, u32[]{:S(2)}) collective-permute-start(bf16[2,4,128]{2,1,0:T(4,128)(2,1)S(1)} %bitcast_reduce_fusion), channel_id=1, source_target_pairs={{0,64},{64,0},{1,65},{65,1},{2,66},{66,2},{3,67},{67,3},{4,68},{68... | collective-permute-start | bytes 6152 | tf_op jit(solution)/shard_map/ppermute | solution.py:430
  31.1 4.4 %copy-start.1 = (bf16[1024,576]{0,1:T(8,128)(2,1)S(1)}, bf16[1024,576]{0,1:T(8,128)(2,1)}, u32[]{:S(2)}) copy-start(bf16[1024,576]{0,1:T(8,128)(2,1)} %param.14) | copy-start | bytes 3538948

commit v7 on v6

--- a/solution.py
+++ b/solution.py
@@ -317,10 +317,15 @@
     field_ref, freq_ref, table_ref, interp_ref, v_ref, s_ref, low_ref, high_ref, last_ref, t_ref
 ):
     freq = lanes_16(freq_ref)
-    placed = jnp.zeros((COLS, 256), F32)
-    for rows in range(ACROSS):
-        source = jnp.concatenate([freq[block(moved(q, rows))] for q in range(8)], axis=0)
-        placed = placed + picked(table_ref, rows, source)
+    sources = [
+        jnp.concatenate([freq[block(moved(q, rows))] for q in range(8)], axis=0)
+        for rows in range(ACROSS)
+    ]
+    placed = jnp.dot(
+        jnp.concatenate(sources, axis=1),
+        table_ref[11, : 16 * ACROSS, :256],
+        preferred_element_type=F32,
+    )
     phases(placed, table_ref, range(HERE), t_ref)
 
     for level in range(3):
@@ -366,8 +371,9 @@
     placed = placed + jnp.dot(across, table_ref[11, :64, 256:512], preferred_element_type=F32)
     phases(placed, table_ref, (HERE, HERE + 1), t_ref)
     v = contribution(s_ref, t_ref, 0, interp_ref[half], w_ref, last_ref)
-    for where, value in ((place, v_ref[...]), (1 - place, v)):
-        part = jnp.dot(value, eval_ref[...], preferred_element_type=F32)
+    both = jnp.concatenate([v_ref[...], v], axis=0)
+    both = jnp.dot(both, eval_ref[...], preferred_element_type=F32)
+    for where, part in ((place, both[:32]), (1 - place, both[32:])):
         part = part.reshape(8, 4, PIX).astype(BF16)
         for p in range(8):
             member = p ^ FLIP_ALL & 7

time: 61.3 us -> 61.1 us (level)
  no operation moved by 1% of the time
where the time goes in v7:
time: 61.1 us; the launch traced here: 60.7 us
  blocking collectives  22.9 us (37%)
  starting transfers between devices  19.7 us (32%)
  Pallas kernels  8.65 us (14%)
  waiting for transfers between devices  5.55 us (9%)
  local copies, waits for them, and re-layouts  3.76 us (6%)
    all_to_all x1, blocking collectives, exchange(): lax.all_to_all(block, axes, split_axis=0, concat_axis=0, tiled=True, axis...  22.9 us
    all_to_all x1, starting transfers between devices, exchange(): lax.all_to_all(block, axes, split_axis=0, concat_axis=0, tiled=True, axis...  12.4 us
    ppermute x1, starting transfers between devices, body(): freq_across = lax.ppermute(spots, 'z4', [(0, 1), (1, 0)])  7.3 us
    all_to_all x1, waiting for transfers between devices, exchange(): lax.all_to_all(block, axes, split_axis=0, concat_axis=0, tiled=True, axis...  5.54 us
    pallas_call x1, Pallas kernels, own_levels(): pl.pallas_call(own_kernel, out_shape=[jax.ShapeDtypeStruct((32, K), BF16)...  4.32 us
    unnamed x12, local copies, waits for them, and re-layouts  2.14 us
    pallas_call x1, Pallas kernels, pack(): pl.pallas_call(pack_kernel, out_shape=jax.ShapeDtypeStruct((32, 4, WIDE),...  2.11 us
    pallas_call x1, Pallas kernels, across_level(): pl.pallas_call(across_kernel, out_shape=jax.ShapeDtypeStruct((2, 8, 8, 4,...  1.6 us
  transfers between devices with their start and end apart: 2, of which 1 were waited for; matrix products, arithmetic and copies ran while one was open for 1% of the time, Pallas kernels for 8%

profile of v7, /device:TPU:1, one launch (start us, length us, event | category | flops | bytes accessed | tf_op | source)
XLA Modules:
  0.0 60.7 jit_solution(4659005356108802469)
XLA Ops:
  0.0 0.0 copy-start.2
  0.0 0.0 copy-start
  0.0 2.1 %pack.1 = bf16[32,4,1280]{2,1,0:T(4,128)(2,1)} custom-call(bf16[1152,128]{1,0:T(8,128)(2,1)} %bitcast.16, bf16[5,2,128]{2,1,0:T(2,128)(2,1)} %bitcast.18), custom_call_target="tpu_custom_call" | custom-call | flops 10000000 | bytes 1048576 | tf_op jit(solution)/shard_map/pack/pallas_call | solution.py:212
  2.1 12.4 %all-to-all-start = ((bf16[32,4,1280]{2,1,0:T(4,128)(2,1)}), bf16[32,4,1280]{2,1,0:T(4,128)(2,1)S(1)}, u32[]{:S(2)}, u32[]{:S(2)}) async-start(bf16[32,4,1280]{2,1,0:T(4,128)(2,1)} %pack.1), calls=%async_computation | async-start | bytes 655360 | tf_op jit(solution)/shard_map/all_to_all | solution.py:427
  14.5 0.9 %reshape.23.nodes_ref = f32[24,576]{1,0:T(8,128)S(1)} reshape(f32[4,3,2,576]{3,2,1,0:T(2,128)} %param.11) | data formatting | bytes 110592 | tf_op jit(solution)/shard_map/reshape | solution.py:437
  15.4 0.0 copy-done.2
  15.4 0.0 copy-start.3
  15.4 0.7 %copy-done.3 = f32[2,24,128]{2,1,0:T(8,128)S(1)} copy-done((f32[2,24,128]{2,1,0:T(8,128)S(1)}, f32[2,24,128]{2,1,0:T(8,128)}, u32[]{:S(2)}) %copy-start.3) | copy-done | bytes 24600
  16.2 0.0 copy-start.4
  16.2 0.7 %copy-done.4 = f32[4,3,2,64]{3,2,1,0:T(2,128)S(1)} copy-done((f32[4,3,2,64]{3,2,1,0:T(2,128)S(1)}, f32[4,3,2,64]{3,2,1,0:T(2,128)}, u32[]{:S(2)}) %copy-start.4) | copy-done | bytes 6168
  16.9 0.0 copy-start.5
  16.9 0.7 %copy-done.5 = f32[8,128]{1,0:T(8,128)S(1)} copy-done((f32[8,128]{1,0:T(8,128)S(1)}, f32[8,128]{1,0:T(8,128)}, u32[]{:S(2)}) %copy-start.5) | copy-done | bytes 4120
  17.5 0.6 %prepare.1.table_ref = bf16[12,96,576]{2,1,0:T(8,128)(2,1)S(1)} custom-call(f32[24,576]{1,0:T(8,128)S(1)} %reshape.23.nodes_ref, f32[24,64]{1,0:T(8,128)S(1)} %bitcast.14, f32[2,24,128]{2,1,0:T(8,128)S(1)} %copy-done.3, f32[8,128]{1,0:T(8,128)S(1)} %copy-done.5, bf16[96,512]{1,0:T(8,128)(2,1)S(1)} %copy-done.2), custom_call_target="tpu_custom_call" | custom-call | flops 10000000 | bytes 5242880 | tf_op jit(solution)/shard_map/prepare/pallas_call | solution.py:163
  18.2 5.5 %all-to-all-done.field_ref = bf16[32,4,1280]{2,1,0:T(4,128)(2,1)S(1)} async-done(((bf16[32,4,1280]{2,1,0:T(4,128)(2,1)}), bf16[32,4,1280]{2,1,0:T(4,128)(2,1)S(1)}, u32[]{:S(2)}, u32[]{:S(2)}) %all-to-all-start) | async-done | bytes 327712 | tf_op jit(solution)/shard_map/all_to_all | solution.py:427
  23.7 7.3 %collective-permute-start = (bf16[2,4,128]{2,1,0:T(4,128)(2,1)S(1)}, bf16[2,4,128]{2,1,0:T(4,128)(2,1)S(1)}, u32[]{:S(2)}, u32[]{:S(2)}) collective-permute-start(bf16[2,4,128]{2,1,0:T(4,128)(2,1)S(1)} %bitcast_reduce_fusion), channel_id=1, source_target_pairs={{0,64},{64,0},{1,65},{65,1},{2,66},{66,2},{3,67},{67,3},{4,68},{68... | collective-permute-start | bytes 6152 | tf_op jit(solution)/shard_map/ppermute | solution.py:436
  31.1 0.0 copy-done
  31.1 0.0 copy-start.1
  31.1 4.3 %own_levels.1 = (bf16[32,576]{1,0:T(8,128)(2,1)S(1)}, f32[256,576]{1,0:T(8,128)S(1)}) custom-call(bf16[32,4,1280]{2,1,0:T(4,128)(2,1)S(1)} %all-to-all-done.field_ref, bf16[32,4,128]{2,1,0:T(4,128)(2,1)S(1)} %slice.4.freq_ref, bf16[12,96,576]{2,1,0:T(8,128)(2,1)S(1)} %prepare.1.table_ref, bf16[2,576,576]{2,1,0:T(8,128)(2,1)S(1)} %copy-done), custom_call_target="tpu_custom_call" | custom-call | flops 1358954496 | bytes 10485760 | tf_op jit(solution)/shard_map/own_levels/pallas_call | solution.py:384
  35.4 0.0 collective-permute-done.freq_across_ref
  35.4 0.0 copy-done.1
  35.4 1.6 %across_level.1 = bf16[2,8,8,4,128]{4,3,2,1,0:T(4,128)(2,1)S(1)} custom-call(bf16[32,4,128]{2,1,0:T(4,128)(2,1)S(1)} %slice.4.freq_ref, bf16[2,4,128]{2,1,0:T(4,128)(2,1)S(1)} %collective-permute-done.freq_across_ref, bf16[32,576]{1,0:T(8,128)(2,1)S(1)} %get-tuple-element.7.v_ref, f32[256,576]{1,0:T(8,128)S(1)} %get-tuple-element.8.s_ref, ...), custom_call_target="tpu_custom_call" | custom-call | flops 339738624 | bytes 5242880 | tf_op jit(solution)/shard_map/across_level/pallas_call | solution.py:407
  37.0 22.9 %all_to_all.10 = bf16[128,4,128]{2,1,0:T(4,128)(2,1)S(1)} all-to-all(bf16[128,4,128]{2,1,0:T(4,128)(2,1)S(1)} %bitcast.13), channel_id=1, replica_groups={{6,7,4,5,2,3,0,1,14,15,12,13,10,11,8,9,22,23,20,21,18,19,16,17,30,31,28..., dimensions={0} | all-to-all | bytes 262144 | tf_op jit(solution)/shard_map/all_to_all | solution.py:427
  59.9 0.1 convert_reduce_fusion
  59.9 0.7 %copy.10 = f32[128,128]{1,0:T(8,128)} copy(f32[128,128]{0,1:T(8,128)S(1)} %bitcast.17) | data formatting | bytes 131072 | tf_op jit(solution)/shard_map/transpose | solution.py:443
  (2 shorter events, 0.0 us)
Async XLA Ops:
  0.0 15.4 %copy-start.2 = (bf16[96,512]{1,0:T(8,128)(2,1)S(1)}, bf16[96,512]{1,0:T(8,128)(2,1)}, u32[]{:S(2)}) copy-start(bf16[96,512]{1,0:T(8,128)(2,1)} %constant.12.clone.pick_ref) | copy-start | bytes 294916
  0.0 31.1 %copy-start = (bf16[2,576,576]{2,1,0:T(8,128)(2,1)S(1)}, bf16[2,576,576]{2,1,0:T(8,128)(2,1)}, u32[]{:S(2)}) copy-start(bf16[2,576,576]{2,1,0:T(8,128)(2,1)} %interp_ref.3) | copy-start | bytes 3981316
  2.1 21.6 %all-to-all-start = ((bf16[32,4,1280]{2,1,0:T(4,128)(2,1)}), bf16[32,4,1280]{2,1,0:T(4,128)(2,1)S(1)}, u32[]{:S(2)}, u32[]{:S(2)}) async-start(bf16[32,4,1280]{2,1,0:T(4,128)(2,1)} %pack.1), calls=%async_computation | async-start | bytes 655360 | tf_op jit(solution)/shard_map/all_to_all | solution.py:427
  15.4 0.7 %copy-start.3 = (f32[2,24,128]{2,1,0:T(8,128)S(1)}, f32[2,24,128]{2,1,0:T(8,128)}, u32[]{:S(2)}) copy-start(f32[2,24,128]{2,1,0:T(8,128)} %constant.10.clone.centre_ref) | copy-start | bytes 73732
  16.2 0.7 %copy-start.4 = (f32[4,3,2,64]{3,2,1,0:T(2,128)S(1)}, f32[4,3,2,64]{3,2,1,0:T(2,128)}, u32[]{:S(2)}) copy-start(f32[4,3,2,64]{3,2,1,0:T(2,128)} %param.12) | copy-start | bytes 18436
  16.9 0.7 %copy-start.5 = (f32[8,128]{1,0:T(8,128)S(1)}, f32[8,128]{1,0:T(8,128)}, u32[]{:S(2)}) copy-start(f32[8,128]{1,0:T(8,128)} %constant.11.clone.mask_ref) | copy-start | bytes 12292
  23.7 11.7 %collective-permute-start = (bf16[2,4,128]{2,1,0:T(4,128)(2,1)S(1)}, bf16[2,4,128]{2,1,0:T(4,128)(2,1)S(1)}, u32[]{:S(2)}, u32[]{:S(2)}) collective-permute-start(bf16[2,4,128]{2,1,0:T(4,128)(2,1)S(1)} %bitcast_reduce_fusion), channel_id=1, source_target_pairs={{0,64},{64,0},{1,65},{65,1},{2,66},{66,2},{3,67},{67,3},{4,68},{68... | collective-permute-start | bytes 6152 | tf_op jit(solution)/shard_map/ppermute | solution.py:436
  31.1 4.3 %copy-start.1 = (bf16[1024,576]{0,1:T(8,128)(2,1)S(1)}, bf16[1024,576]{0,1:T(8,128)(2,1)}, u32[]{:S(2)}) copy-start(bf16[1024,576]{0,1:T(8,128)(2,1)} %param.14) | copy-start | bytes 3538948

commit v8 on v7

--- a/solution.py
+++ b/solution.py
@@ -429,6 +429,26 @@
     )
 
 
+def finish_kernel(part_ref, out_ref):
+    total = jnp.zeros((8, 4, 4, 128), F32)
+    for z4 in range(2):
+        for zh in range(2):
+            total = total + part_ref[z4, :, zh].astype(F32)
+    out_ref[...] = total.reshape(COLS, 128).T
+
+
+def finish(part):
+    return pl.pallas_call(
+        finish_kernel,
+        out_shape=jax.ShapeDtypeStruct((128, COLS), F32),
+        in_specs=[VMEM],
+        out_specs=VMEM,
+        compiler_params=pltpu.CompilerParams(vmem_limit_bytes=4 * 2**20),
+        cost_estimate=pl.CostEstimate(flops=10**5, bytes_accessed=2**18, transcendentals=0),
+        name="finish",
+    )(part)
+
+
 def body(coeffs, freqs, nodes, centres, interp, evaluate):
     field = exchange(pack(coeffs.reshape(2 * K, COLS), freqs[0]), NEAR, FLIP_NEAR)
     freq = field[:, :, WIDE - 128 :]
@@ -439,8 +459,7 @@
     part = across_level(freq, freq_across, v, state, table, interp, evaluate.T)
     part = part.reshape(128, 4, 128)
     part = exchange(part, ALL, FLIP_ALL)
-    total = jnp.sum(part.reshape(2, 8, 2, 4, 4, 128).astype(F32), axis=(0, 2))
-    return total.reshape(COLS, 128).T
+    return finish(part.reshape(2, 8, 2, 4, 4, 128))
 
 
 def solution(mesh):

time: 61.1 us -> 61.1 us (level)
  Pallas kernels: 8.65 us -> 9.41 us
  local copies, waits for them, and re-layouts: 3.76 us -> 3.03 us
    pallas_call x0 -> x1, Pallas kernels: none -> 0.73 us  [finish(): pl.pallas_call(finish_kernel, out_shape=jax.ShapeDtypeStruct((128, COLS),...]
    transpose x1 -> x0, local copies, waits for them, and re-layouts: 0.73 us -> none  [body(): return total.reshape(COLS, 128).T]
where the time goes in v8:
time: 61.1 us; the launch traced here: 60.6 us
  blocking collectives  22.9 us (37%)
  starting transfers between devices  19.7 us (32%)
  Pallas kernels  9.41 us (15%)
  waiting for transfers between devices  5.55 us (9%)
  local copies, waits for them, and re-layouts  3.03 us (5%)
    all_to_all x1, blocking collectives, exchange(): lax.all_to_all(block, axes, split_axis=0, concat_axis=0, tiled=True, axis...  22.9 us
    all_to_all x1, starting transfers between devices, exchange(): lax.all_to_all(block, axes, split_axis=0, concat_axis=0, tiled=True, axis...  12.4 us
    ppermute x1, starting transfers between devices, body(): freq_across = lax.ppermute(spots, 'z4', [(0, 1), (1, 0)])  7.3 us
    all_to_all x1, waiting for transfers between devices, exchange(): lax.all_to_all(block, axes, split_axis=0, concat_axis=0, tiled=True, axis...  5.55 us
    pallas_call x1, Pallas kernels, own_levels(): pl.pallas_call(own_kernel, out_shape=[jax.ShapeDtypeStruct((32, K), BF16)...  4.33 us
    unnamed x12, local copies, waits for them, and re-layouts  2.14 us
    pallas_call x1, Pallas kernels, pack(): pl.pallas_call(pack_kernel, out_shape=jax.ShapeDtypeStruct((32, 4, WIDE),...  2.12 us
    pallas_call x1, Pallas kernels, across_level(): pl.pallas_call(across_kernel, out_shape=jax.ShapeDtypeStruct((2, 8, 8, 4,...  1.6 us
  transfers between devices with their start and end apart: 2, of which 1 were waited for; matrix products, arithmetic and copies ran while one was open for 1% of the time, Pallas kernels for 8%

profile of v8, /device:TPU:1, one launch (start us, length us, event | category | flops | bytes accessed | tf_op | source)
XLA Modules:
  0.0 60.6 jit_solution(3780573810962819343)
XLA Ops:
  0.0 0.0 copy-start.2
  0.0 0.0 copy-start
  0.0 2.1 %pack.1 = bf16[32,4,1280]{2,1,0:T(4,128)(2,1)} custom-call(bf16[1152,128]{1,0:T(8,128)(2,1)} %bitcast.12, bf16[5,2,128]{2,1,0:T(2,128)(2,1)} %bitcast.13), custom_call_target="tpu_custom_call" | custom-call | flops 10000000 | bytes 1048576 | tf_op jit(solution)/shard_map/pack/pallas_call | solution.py:212
  2.1 12.4 %all-to-all-start = ((bf16[32,4,1280]{2,1,0:T(4,128)(2,1)}), bf16[32,4,1280]{2,1,0:T(4,128)(2,1)S(1)}, u32[]{:S(2)}, u32[]{:S(2)}) async-start(bf16[32,4,1280]{2,1,0:T(4,128)(2,1)} %pack.1), calls=%async_computation | async-start | bytes 655360 | tf_op jit(solution)/shard_map/all_to_all | solution.py:427
  14.5 0.9 %reshape.20.nodes_ref = f32[24,576]{1,0:T(8,128)S(1)} reshape(f32[4,3,2,576]{3,2,1,0:T(2,128)} %param.11) | data formatting | bytes 110592 | tf_op jit(solution)/shard_map/reshape | solution.py:457
  15.4 0.0 copy-done.2
  15.4 0.0 copy-start.3
  15.4 0.7 %copy-done.3 = f32[2,24,128]{2,1,0:T(8,128)S(1)} copy-done((f32[2,24,128]{2,1,0:T(8,128)S(1)}, f32[2,24,128]{2,1,0:T(8,128)}, u32[]{:S(2)}) %copy-start.3) | copy-done | bytes 24600
  16.2 0.0 copy-start.4
  16.2 0.7 %copy-done.4 = f32[4,3,2,64]{3,2,1,0:T(2,128)S(1)} copy-done((f32[4,3,2,64]{3,2,1,0:T(2,128)S(1)}, f32[4,3,2,64]{3,2,1,0:T(2,128)}, u32[]{:S(2)}) %copy-start.4) | copy-done | bytes 6168
  16.9 0.0 copy-start.5
  16.9 0.7 %copy-done.5 = f32[8,128]{1,0:T(8,128)S(1)} copy-done((f32[8,128]{1,0:T(8,128)S(1)}, f32[8,128]{1,0:T(8,128)}, u32[]{:S(2)}) %copy-start.5) | copy-done | bytes 4120
  17.6 0.6 %prepare.1.table_ref = bf16[12,96,576]{2,1,0:T(8,128)(2,1)S(1)} custom-call(f32[24,576]{1,0:T(8,128)S(1)} %reshape.20.nodes_ref, f32[24,64]{1,0:T(8,128)S(1)} %bitcast.11, f32[2,24,128]{2,1,0:T(8,128)S(1)} %copy-done.3, f32[8,128]{1,0:T(8,128)S(1)} %copy-done.5, bf16[96,512]{1,0:T(8,128)(2,1)S(1)} %copy-done.2), custom_call_target="tpu_custom_call" | custom-call | flops 10000000 | bytes 5242880 | tf_op jit(solution)/shard_map/prepare/pallas_call | solution.py:163
  18.2 5.5 %all-to-all-done.field_ref = bf16[32,4,1280]{2,1,0:T(4,128)(2,1)S(1)} async-done(((bf16[32,4,1280]{2,1,0:T(4,128)(2,1)}), bf16[32,4,1280]{2,1,0:T(4,128)(2,1)S(1)}, u32[]{:S(2)}, u32[]{:S(2)}) %all-to-all-start) | async-done | bytes 327712 | tf_op jit(solution)/shard_map/all_to_all | solution.py:427
  23.8 7.3 %collective-permute-start = (bf16[2,4,128]{2,1,0:T(4,128)(2,1)S(1)}, bf16[2,4,128]{2,1,0:T(4,128)(2,1)S(1)}, u32[]{:S(2)}, u32[]{:S(2)}) collective-permute-start(bf16[2,4,128]{2,1,0:T(4,128)(2,1)S(1)} %bitcast_reduce_fusion), channel_id=1, source_target_pairs={{0,64},{64,0},{1,65},{65,1},{2,66},{66,2},{3,67},{67,3},{4,68},{68... | collective-permute-start | bytes 6152 | tf_op jit(solution)/shard_map/ppermute | solution.py:456
  31.1 0.0 copy-done
  31.1 0.0 copy-start.1
  31.1 4.3 %own_levels.1 = (bf16[32,576]{1,0:T(8,128)(2,1)S(1)}, f32[256,576]{1,0:T(8,128)S(1)}) custom-call(bf16[32,4,1280]{2,1,0:T(4,128)(2,1)S(1)} %all-to-all-done.field_ref, bf16[32,4,128]{2,1,0:T(4,128)(2,1)S(1)} %slice.4.freq_ref, bf16[12,96,576]{2,1,0:T(8,128)(2,1)S(1)} %prepare.1.table_ref, bf16[2,576,576]{2,1,0:T(8,128)(2,1)S(1)} %copy-done), custom_call_target="tpu_custom_call" | custom-call | flops 1358954496 | bytes 10485760 | tf_op jit(solution)/shard_map/own_levels/pallas_call | solution.py:384
  35.4 0.0 collective-permute-done.freq_across_ref
  35.4 0.0 copy-done.1
  35.4 1.6 %across_level.1 = bf16[2,8,8,4,128]{4,3,2,1,0:T(4,128)(2,1)S(1)} custom-call(bf16[32,4,128]{2,1,0:T(4,128)(2,1)S(1)} %slice.4.freq_ref, bf16[2,4,128]{2,1,0:T(4,128)(2,1)S(1)} %collective-permute-done.freq_across_ref, bf16[32,576]{1,0:T(8,128)(2,1)S(1)} %get-tuple-element.7.v_ref, f32[256,576]{1,0:T(8,128)S(1)} %get-tuple-element.8.s_ref, ...), custom_call_target="tpu_custom_call" | custom-call | flops 339738624 | bytes 5242880 | tf_op jit(solution)/shard_map/across_level/pallas_call | solution.py:407
  37.1 22.9 %all_to_all.10 = bf16[128,4,128]{2,1,0:T(4,128)(2,1)S(1)} all-to-all(bf16[128,4,128]{2,1,0:T(4,128)(2,1)S(1)} %bitcast.9), channel_id=1, replica_groups={{6,7,4,5,2,3,0,1,14,15,12,13,10,11,8,9,22,23,20,21,18,19,16,17,30,31,28..., dimensions={0} | all-to-all | bytes 262144 | tf_op jit(solution)/shard_map/all_to_all | solution.py:427
  59.9 0.7 %finish.1 = f32[128,128]{1,0:T(8,128)} custom-call(bf16[2,8,2,4,4,128]{5,4,3,2,1,0:T(4,128)(2,1)S(1)} %bitcast.10), custom_call_target="tpu_custom_call" | custom-call | flops 100000 | bytes 262144 | tf_op jit(solution)/shard_map/finish/pallas_call | solution.py:441
  (2 shorter events, 0.0 us)
Async XLA Ops:
  0.0 15.4 %copy-start.2 = (bf16[96,512]{1,0:T(8,128)(2,1)S(1)}, bf16[96,512]{1,0:T(8,128)(2,1)}, u32[]{:S(2)}) copy-start(bf16[96,512]{1,0:T(8,128)(2,1)} %constant.11.clone.pick_ref) | copy-start | bytes 294916
  0.0 31.1 %copy-start = (bf16[2,576,576]{2,1,0:T(8,128)(2,1)S(1)}, bf16[2,576,576]{2,1,0:T(8,128)(2,1)}, u32[]{:S(2)}) copy-start(bf16[2,576,576]{2,1,0:T(8,128)(2,1)} %interp_ref.3) | copy-start | bytes 3981316
  2.1 21.6 %all-to-all-start = ((bf16[32,4,1280]{2,1,0:T(4,128)(2,1)}), bf16[32,4,1280]{2,1,0:T(4,128)(2,1)S(1)}, u32[]{:S(2)}, u32[]{:S(2)}) async-start(bf16[32,4,1280]{2,1,0:T(4,128)(2,1)} %pack.1), calls=%async_computation | async-start | bytes 655360 | tf_op jit(solution)/shard_map/all_to_all | solution.py:427
  15.4 0.7 %copy-start.3 = (f32[2,24,128]{2,1,0:T(8,128)S(1)}, f32[2,24,128]{2,1,0:T(8,128)}, u32[]{:S(2)}) copy-start(f32[2,24,128]{2,1,0:T(8,128)} %constant.9.clone.centre_ref) | copy-start | bytes 73732
  16.2 0.7 %copy-start.4 = (f32[4,3,2,64]{3,2,1,0:T(2,128)S(1)}, f32[4,3,2,64]{3,2,1,0:T(2,128)}, u32[]{:S(2)}) copy-start(f32[4,3,2,64]{3,2,1,0:T(2,128)} %param.12) | copy-start | bytes 18436
  16.9 0.7 %copy-start.5 = (f32[8,128]{1,0:T(8,128)S(1)}, f32[8,128]{1,0:T(8,128)}, u32[]{:S(2)}) copy-start(f32[8,128]{1,0:T(8,128)} %constant.10.clone.mask_ref) | copy-start | bytes 12292
  23.8 11.7 %collective-permute-start = (bf16[2,4,128]{2,1,0:T(4,128)(2,1)S(1)}, bf16[2,4,128]{2,1,0:T(4,128)(2,1)S(1)}, u32[]{:S(2)}, u32[]{:S(2)}) collective-permute-start(bf16[2,4,128]{2,1,0:T(4,128)(2,1)S(1)} %bitcast_reduce_fusion), channel_id=1, source_target_pairs={{0,64},{64,0},{1,65},{65,1},{2,66},{66,2},{3,67},{67,3},{4,68},{68... | collective-permute-start | bytes 6152 | tf_op jit(solution)/shard_map/ppermute | solution.py:456
  31.1 4.3 %copy-start.1 = (bf16[1024,576]{0,1:T(8,128)(2,1)S(1)}, bf16[1024,576]{0,1:T(8,128)(2,1)}, u32[]{:S(2)}) copy-start(bf16[1024,576]{0,1:T(8,128)(2,1)} %param.14) | copy-start | bytes 3538948
